TPU v7x, 512 devices: a whole 4x8x8 slice. The times are simulated.
512 devices in a mesh: blk: 128 (over y_lo, x, z), grp: 4 (over y_hi, core).
Axes of the slice: x: 4, y: 8 (y_hi: 2, y_lo: 4; y = y_hi * 4 + y_lo), z: 8, core: 2. Of those that a mesh axis runs over, the one named last changes fastest.
Arguments:
- queries: bfloat16 [65536, 1024], P(('blk', 'grp')), may hold values from -16 to 16
- passages: bfloat16 [2048, 1024], P(('blk', 'grp')), may hold values from -16 to 16
- negatives: bfloat16 [458752, 1024], P(('blk', 'grp')), may hold values from -16 to 16
- neg_ids: int32 [65536, 7], P(('blk', 'grp')), may hold values from 0 to 458751, as said below
- positives: int32 [65536], P(('blk', 'grp')), may hold values from 0 to 2047
Outputs:
- grad_queries: float32 [65536, 1024], P(('blk', 'grp'))
- grad_passages: float32 [2048, 1024], P(('blk', 'grp'))
Inputs may be any that keep to these rules, and one draw needn't show every extreme that they name: The row neg_ids[i, k] lies on a device of the same grp index as query i's device (rows are laid out 896 a device along blk+grp); of one device's queries at most 10 ids fall on any one device, and for every device there is some device on which exactly 10 of its ids fall.
All inputs are finite; a program needn't handle non-finite values.
Results may differ from a plain program's by a relative error of at most 0.0015.
Values may be sent and summed in bfloat16 or wider, within the bound.
A program may use at most 64 MiB of HBM per device.

v0:
```python
import math

import jax
import jax.numpy as jnp
from jax import lax
from jax.sharding import PartitionSpec as P


def joined(part, axis, combine):
    gathered = jax.tree.map(lambda a: lax.all_gather(a, axis), part)

    def take(source):
        return jax.tree.map(lambda a: lax.dynamic_index_in_dim(a, source, 0, False), gathered)

    return lax.fori_loop(
        1, lax.axis_size(axis), lambda source, state: combine(state, take(source)), take(0)
    )


def cross_dot(left, right):
    return lax.dot_general(
        left, right, (((1,), (1,)), ((), ())), preferred_element_type=jnp.float32
    )


def merge_pair(first, second):
    top_score = jnp.maximum(first[0], second[0])
    return (
        top_score,
        first[1] * jnp.exp(first[0] - top_score) + second[1] * jnp.exp(second[0] - top_score),
    )


def shards(queries, passages, negatives, neg_ids, positives):
    width = queries.shape[1]
    score_scale = 3.0 / math.sqrt(width)
    q_count = queries.shape[0]
    p_count = passages.shape[0]
    table_rows = negatives.shape[0]
    hard_count = neg_ids.shape[1]
    blk_size = lax.axis_size("blk")
    grp_size = lax.axis_size("grp")
    grp_index = lax.axis_index("grp")
    offset = grp_index * q_count
    pool_rows = blk_size * p_count
    block_q, block_answer = (
        lax.all_gather(queries, "grp", axis=0, tiled=True),
        lax.all_gather(positives, "grp", axis=0, tiled=True),
    )
    block_rows = block_q.shape[0]
    flat_ids = neg_ids.reshape(-1)
    owners = flat_ids // table_rows // grp_size
    local_rows = flat_ids % table_rows
    owner_hot = (owners[:, None] == jnp.arange(blk_size, dtype=jnp.int32)[None, :]).astype(
        jnp.int32
    )
    ranks = jnp.sum(jnp.cumsum(owner_hot, axis=0) * owner_hot, axis=1) - 1
    capacity = hard_count * q_count // blk_size + 3
    requests = jnp.zeros((blk_size, capacity), jnp.int32).at[owners, ranks].set(local_rows)
    found = negatives[lax.all_to_all(requests, "blk", split_axis=0, concat_axis=0, tiled=True)]
    fetched = lax.all_to_all(found, "blk", split_axis=0, concat_axis=0, tiled=True)
    hard_rows = fetched[owners, ranks].reshape(q_count, hard_count, width)
    hard_scores = (
        jnp.einsum("qd,qkd->qk", queries, hard_rows, preferred_element_type=jnp.float32)
        * score_scale
    )
    start_top = jnp.full((block_rows,), -1e30, jnp.float32)
    scores = cross_dot(block_q, lax.all_gather(passages, "blk", axis=0, tiled=True)) * score_scale
    new_top = jnp.maximum(start_top, jnp.max(scores, axis=1))
    totals = jnp.sum(jnp.exp(scores - new_top[:, None]), axis=1)
    top_score, totals = (new_top, totals)
    column = lax.all_gather(passages, "blk", axis=0, tiled=True)
    hard_top = jnp.max(hard_scores, axis=1)
    hard_total = jnp.sum(jnp.exp(hard_scores - hard_top[:, None]), axis=1)
    hard_top_full = lax.dynamic_update_slice_in_dim(
        jnp.full((block_rows,), -1e30, jnp.float32), hard_top, offset, 0
    )
    hard_total_full = lax.dynamic_update_slice_in_dim(
        jnp.zeros((block_rows,), jnp.float32), hard_total, offset, 0
    )
    local_pair = merge_pair((top_score, totals), (hard_top_full, hard_total_full))
    merged_top, merged_total = joined(local_pair, "grp", merge_pair)
    lse = merged_top + jnp.log(merged_total)
    scores = cross_dot(block_q, column) * score_scale
    in_column = block_answer // p_count % grp_size == grp_index
    column_slot = block_answer // (p_count * grp_size) * p_count + block_answer % p_count
    answer_hot = (
        in_column[:, None]
        & (column_slot[:, None] == jnp.arange(pool_rows, dtype=jnp.int32)[None, :])
    ).astype(jnp.float32)
    weights = (jnp.exp(scores - lse[:, None]) - answer_hot).astype(jnp.bfloat16)
    part_weights = weights
    grad_passages = (
        lax.psum_scatter(
            lax.dot_general(
                part_weights, block_q, (((0,), (0,)), ((), ())), preferred_element_type=jnp.float32
            ),
            "blk",
            scatter_dimension=0,
            tiled=True,
        )
        * score_scale
    )
    own_lse = lax.dynamic_slice_in_dim(lse, offset, q_count, 0)
    part_weights = weights
    grad_sum = lax.psum_scatter(
        jnp.dot(part_weights, column, preferred_element_type=jnp.float32),
        "grp",
        scatter_dimension=0,
        tiled=True,
    )
    hard_weights = jnp.exp(hard_scores - own_lse[:, None]).astype(jnp.bfloat16)
    grad_sum = grad_sum + jnp.einsum(
        "qk,qkd->qd", hard_weights, hard_rows, preferred_element_type=jnp.float32
    )
    return (grad_sum * score_scale, grad_passages)


def solution(mesh):
    in_specs = (
        P(("blk", "grp"), None),
        P(("blk", "grp"), None),
        P(("blk", "grp"), None),
        P(("blk", "grp"), None),
        P(("blk", "grp")),
    )
    out_specs = (P(("blk", "grp"), None), P(("blk", "grp"), None))
    return jax.shard_map(shards, mesh=mesh, in_specs=in_specs, out_specs=out_specs, check_vma=False)
```

profile of v0, /device:TPU:1, one launch (start us, length us, event | category | flops | bytes accessed | tf_op | source)
XLA Modules:
  0.0 2404.1 jit_solution(5429113511414245156)
XLA Ops:
  11.7 46.3 %scatter_fusion = s32[128,10]{0,1:T(8,128)S(1)} fusion(s32[128,10]{0,1:T(8,128)S(1)} %broadcast.273, s32[896]{0:T(1024)S(1)} %get-tuple-element.138, s32[896]{0:T(1024)S(1)} %get-tuple-element.157), kind=kCustom, calls=%fused_computation.2 | custom fusion | bytes 17920 | tf_op jit(solution)/shard_map/scatter | solution.py:59
  58.1 29.5 %all_to_all.17 = s32[128,1,10]{2,1,0:T(1,128)S(1)} all-to-all(s32[128,1,10]{2,1,0:T(1,128)S(1)} %copy.39), channel_id=1, replica_groups=mesh['blk'=128,'grp'=4] {'blk'}, dimensions={0} | all-to-all | bytes 10240 | tf_op jit(solution)/shard_map/all_to_all | solution.py:60
  87.8 5.1 gather_fusion
  92.9 6.0 reshape.219
  98.8 7.5 all-to-all-start.1
  107.9 71.4 %all-gather.5 = s32[4,1,128]{2,1,0:T(1,128)S(1)} all-gather(s32[1,1,128]{2,1,0:T(1,128)S(1)} %bitcast.72), channel_id=1, replica_groups=mesh['blk'=128,'grp'=4] {'grp'}, dimensions={0}, use_global_device_ids=true | all-gather | bytes 2560 | tf_op jit(solution)/shard_map/all_gather | solution.py:48
  179.4 575.1 %all-gather.11.cloned.1.call-done = bf16[128,4,1024]{2,1,0:T(4,128)(2,1)} async-done(((bf16[1,4,1024]{2,1,0:T(4,128)(2,1)}), bf16[128,4,1024]{2,1,0:T(4,128)(2,1)}) %all-gather.11.cloned.1.call-update) | async-done | bytes 1048592 | tf_op jit(solution)/shard_map/all_gather | solution.py:72
  754.5 2.2 reshape.246
  756.7 112.5 %all-gather.9.cloned.1.call-done = bf16[512,1024]{1,0:T(8,128)(2,1)} async-done(((bf16[128,1024]{1,0:T(8,128)(2,1)}), bf16[512,1024]{1,0:T(8,128)(2,1)}) %all-gather.9.cloned.1.call-update) | async-done | bytes 1048592 | tf_op jit(solution)/shard_map/all_gather | solution.py:47
  869.3 2.3 fusion.26
  871.8 5.2 copy.40
  876.9 18.9 gather_fusion.1
  895.9 3.9 reshape.217
  899.8 2.8 fusion.2
  903.2 9.1 all-gather.3
  912.4 9.1 all-gather.4
  921.6 3.3 fusion.24
  925.0 3.4 fusion.25
  928.4 1.3 dynamic-slice
  930.6 2.3 fusion.27
  932.9 1317.8 %all-reduce.3.cloned.1.call-done = f32[512,1024]{1,0:T(8,128)} async-done(((f32[512,1024]{1,0:T(8,128)}), f32[512,1024]{1,0:T(8,128)}) %all-reduce.3.cloned.1.call-update) | async-done | bytes 2097168
  2250.7 1.4 dynamic-slice_multiply_fusion
  2252.0 143.6 %reduce-scatter.2.cloned.1.call-done = f32[128,1024]{1,0:T(8,128)} async-done(((f32[512,1024]{1,0:T(8,128)}), f32[128,1024]{1,0:T(8,128)}) %reduce-scatter.2.cloned.1.call-update) | async-done | bytes 524304 | tf_op jit(solution)/shard_map/reduce_scatter | solution.py:106
  2395.6 2.0 fusion.1
  (71 shorter events, 7.6 us)
Async XLA Ops:
  7.2 80.6 %copy-start = (bf16[896,1024]{1,0:T(8,128)(2,1)S(1)}, bf16[896,1024]{1,0:T(8,128)(2,1)}, u32[]{:S(2)}) copy-start(bf16[896,1024]{1,0:T(8,128)(2,1)} %param.9) | copy-start | bytes 5505028
  98.8 9.1 copy-start.2
  98.8 772.9 %all-to-all-start.1 = ((bf16[128,10,1024]{2,1,0:T(8,128)(2,1)}), bf16[128,10,1024]{2,1,0:T(8,128)(2,1)}, u32[]{:S(2)}, u32[]{:S(2)}) async-start(bf16[128,10,1024]{2,1,0:T(8,128)(2,1)} %reshape.219), calls=%async_computation.1 | async-start | bytes 8388608 | tf_op jit(solution)/shard_map/all_to_all | solution.py:61
  106.4 648.1 %all-gather.11.cloned.1.call-start = ((), (), s32[]{:S(2)}) async-start(), calls=%async_computation.5 | async-start | bytes 1056768 | tf_op jit(solution)/shard_map/all_gather | solution.py:72
  107.1 762.2 %all-gather.9.cloned.1.call-start = ((), (), s32[]{:S(2)}) async-start(), calls=%async_computation.3 | async-start | bytes 1310720 | tf_op jit(solution)/shard_map/all_gather | solution.py:47
  107.9 2142.8 %all-reduce.3.cloned.1.call-start = ((), (), s32[]{:S(2)}) async-start(), calls=%async_computation.6 | async-start | bytes 4194304
  895.9 3.9 copy-start.1
  925.0 1470.7 %reduce-scatter.2.cloned.1.call-start = ((), (), s32[]{:S(2)}) async-start(), calls=%async_computation.4 | async-start | bytes 2621440 | tf_op jit(solution)/shard_map/reduce_scatter | solution.py:106
Sparse Core Ops, SparseCore 0:
  109.3 645.1 all-gather.10
  756.6 112.6 all-gather.8
  925.1 1325.5 all-reduce.2
  2253.9 141.6 reduce-scatter.1
where the time goes:
time: 2410 us; the launch traced here: 2400 us
  waiting for transfers between devices  2150 us (89%)
  blocking collectives  119 us (5%)
  local copies, waits for them, and re-layouts  92.1 us (4%)
    unnamed x5, waiting for transfers between devices  1320 us
    all_gather x1, waiting for transfers between devices, shards(): column = lax.all_gather(passages, 'blk', axis=0, tiled=True)  575 us
    reduce_scatter x1, waiting for transfers between devices, shards(): lax.psum_scatter(jnp.dot(part_weights, column, preferred_element_type=jnp...  144 us
    all_gather x1, waiting for transfers between devices, shards(): lax.all_gather(queries, 'grp', axis=0, tiled=True)  113 us
    all_gather x1, blocking collectives, shards(): lax.all_gather(positives, 'grp', axis=0, tiled=True)  71.4 us
  transfers between devices with their start and end apart: 5, of which 4 were waited for; matrix products, arithmetic and copies ran while one was open for 1% of the time, Pallas kernels for 0%

commit v1 on v0

v1 whole, which is shorter than its diff:
```python
import functools
import math

import jax
import jax.numpy as jnp
from jax import lax
from jax.experimental import pallas as pl
from jax.experimental.pallas import tpu as pltpu
from jax.sharding import PartitionSpec as P

MESH = pl.DeviceIdType.MESH
F32, BF16, I32 = jnp.float32, jnp.bfloat16, jnp.int32

NX, NY, NZ, NYL = 4, 8, 8, 4
NB = 128
MUL, INV = 37, 45
CAP = 10
Q, D, HARD, ROWS = 128, 1024, 7, 896
C8 = D // 128
SLAB = CAP * C8
GROUPS = 8
PER = NB // GROUPS
SLOTS = NB * CAP
NP = 2048
SCALE = 3.0 / math.sqrt(D)
NEG = -1e30


def device(x, y, z, core):
    return (((y % NYL) * NX + x) * NZ + z, (y // NYL) * 2 + core)


def rcopy(src, dst, send, recv, dev):
    return pltpu.make_async_remote_copy(
        src_ref=src, dst_ref=dst, send_sem=send, recv_sem=recv, device_id=dev, device_id_type=MESH
    )


def nt(left, right):
    return lax.dot_general(left, right, (((1,), (1,)), ((), ())), preferred_element_type=F32)


def mm(left, right):
    return lax.dot_general(left, right, (((1,), (0,)), ((), ())), preferred_element_type=F32)


def iota(shape, dim):
    return lax.broadcasted_iota(I32, shape, dim)


def requests(ids_ref, req, slots):
    mb = lax.axis_index("blk")
    yl, x, z = mb // (NX * NZ), (mb // NZ) % NX, mb % NZ

    lane = iota((Q, 128), 1)
    lower = (iota((Q, Q), 0) > iota((Q, Q), 1)).astype(F32).astype(BF16)
    base = jnp.zeros((1, 128), F32)
    want_hi = jnp.zeros((NB, 128), F32)
    want_lo = jnp.zeros((NB, 128), F32)
    slot_cols = jnp.full((Q, 128), -1.0, F32)
    for k in range(HARD):
        ids = ids_ref[:, k:k + 1]
        dev = jnp.floor((ids.astype(F32) + 0.5) * (1.0 / ROWS)).astype(I32)
        row = ids - dev * ROWS
        owner = dev >> 2
        off = (
            (((yl - (owner >> 5)) & 3) << 5)
            | (((x - ((owner >> 3) & 3)) & 3) << 3)
            | ((z - (owner & 7)) & 7)
        )
        step = (off * INV) & (NB - 1)
        hot = (lane == step).astype(F32)
        rank = jnp.sum(hot * (mm(lower, hot.astype(BF16)) + base), axis=1, keepdims=True)
        base = base + jnp.sum(hot, axis=0, keepdims=True)
        slot_cols = jnp.where(lane == k, step.astype(F32) * CAP + rank, slot_cols)
        at_rank = (lane.astype(F32) == rank).astype(F32)
        hot_t = jnp.transpose(hot).astype(BF16)
        want_hi = want_hi + mm(hot_t, (at_rank * (row >> 3).astype(F32)).astype(BF16))
        want_lo = want_lo + mm(hot_t, (at_rank * (row & 7).astype(F32)).astype(BF16))
    want = (want_hi * 8.0 + want_lo).astype(I32)
    req[...] = want.reshape(NB, 1, 128)
    slots[...] = jnp.transpose(slot_cols).astype(I32)


def kernel(
    req, slots, pos_ref, pas_ref, q_ref, neg_ref,
    gq_ref, gp_ref,
    reqin, idsm, tab, g, f, fs, fn, st, hs, pst, pmine, zbuf, zf, pall,
    wt, gpb, rc, r1x, r1a, ax, aa, r2x, r2a, a3, r3,
    s_req, s_row, s_ag, r_req, r_row, r_ag, s_rc, r_rc, s_1, r_1, s_2, r_2, s_3, r_3, s_loc,
):
    mb = lax.axis_index("blk")
    mg = lax.axis_index("grp")
    yl, x, z = mb // (NX * NZ), (mb // NZ) % NX, mb % NZ
    yh, core = mg // 2, mg % 2
    y = yh * NYL + yl

    def shifted(step, sign):
        k = (step * MUL) % NB
        ky, kx, kz = k // (NX * NZ), (k // NZ) % NX, k % NZ
        py = (yl + NYL + sign * ky) % NYL
        px = (x + NX + sign * kx) % NX
        pz = (z + NZ + sign * kz) % NZ
        return ((py * NX + px) * NZ + pz, mg)

    sibling = device(x, y, z, 1 - core)

    barrier = pltpu.get_barrier_semaphore()

    def greet(step, _):
        pl.semaphore_signal(barrier, inc=1, device_id=shifted(step, 1), device_id_type=MESH)
        return 0

    lax.fori_loop(1, NB, greet, 0)
    for i in range(NYL):
        other = device(x, (1 - yh) * NYL + i, z, core)
        pl.semaphore_signal(barrier, inc=1, device_id=other, device_id_type=MESH)
    pl.semaphore_signal(barrier, inc=1, device_id=sibling, device_id_type=MESH)

    for c in range(C8):
        pst[pl.ds(c, 4, stride=C8), :] = pas_ref[:, c * 128:(c + 1) * 128].astype(F32)
    own = pst[...].astype(BF16)
    pmine[...] = own
    zbuf[z] = own

    pl.semaphore_wait(barrier, NB - 1 + NYL + 1)

    def ask(step, _):
        rcopy(req.at[step], reqin.at[step], s_req, r_req, shifted(step, -1)).start()
        return 0

    lax.fori_loop(1, NB, ask, 0)
    reqin[0] = req[0]

    for i in range(1, NZ):
        to = device(x, y, (z + i) % NZ, core)
        rcopy(pmine, zbuf.at[z], s_ag.at[0], r_ag.at[0], to).start()

    flat = tab.reshape(ROWS * C8, 128)
    for t in range(ROWS // 128):
        for c in range(C8):
            part = neg_ref[t * 128:(t + 1) * 128, c * 128:(c + 1) * 128].astype(F32)
            flat[pl.ds(t * 1024 + c, 128, stride=C8), :] = part

    rcopy(zbuf.at[pl.ds(0, NZ - 1)], zbuf.at[pl.ds(0, NZ - 1)], s_ag.at[0], r_ag.at[0], sibling).wait_recv()
    zf[...] = zbuf[...].reshape(NZ * 32, 128).astype(F32)
    mine = pl.multiple_of(((core * NX + x) * NY + y) * 32, 32)
    for c in range(C8):
        pall[pl.ds(mine, 32), c * 128:(c + 1) * 128] = zf[pl.ds(c, 32, stride=C8), :].astype(BF16)

    for i in range(1, NY):
        to = device(x, (y + i) % NY, z, core)
        block = pall.at[pl.ds(mine, 32)]
        rcopy(block, block, s_ag.at[1], r_ag.at[1], to).start()

    rcopy(reqin.at[pl.ds(0, NB - 1)], reqin.at[pl.ds(0, NB - 1)], s_req, r_req, sibling).wait_recv()
    local = pltpu.make_async_copy(reqin, idsm, s_loc)
    local.start()
    local.wait()

    def pick(step, dst):
        at = pl.multiple_of(step * SLAB, 16)
        for j in range(CAP // 2):
            pair = jnp.concatenate([tab[idsm[step, 0, 2 * j]], tab[idsm[step, 0, 2 * j + 1]]], axis=0)
            dst[pl.ds(at + 16 * j, 16), :] = pair.astype(BF16)

    def answer(step, _):
        pick(step, g)
        at = pl.multiple_of(step * SLAB, 16)
        rcopy(
            g.at[pl.ds(at, SLAB)], f.at[pl.ds(at, SLAB)], s_row, r_row.at[step // PER], shifted(step, 1)
        ).start()
        return 0

    lax.fori_loop(1, NB, answer, 0)
    pick(0, f)

    rcopy(pall.at[pl.ds(0, 224)], pall.at[pl.ds(0, 224)], s_ag.at[1], r_ag.at[1], sibling).wait_recv()
    for i in range(1, NX):
        to = device((x + i) % NX, y, z, core)
        block = pall.at[pl.ds(pl.multiple_of((core * NX + x) * 256, 256), 256)]
        rcopy(block, block, s_ag.at[2], r_ag.at[2], to).start()
    rcopy(pall.at[pl.ds(0, 768)], pall.at[pl.ds(0, 768)], s_ag.at[2], r_ag.at[2], sibling).wait_recv()
    half = pall.at[pl.ds(pl.multiple_of(core * 1024, 1024), 1024)]
    rcopy(half, half, s_ag.at[3], r_ag.at[3], sibling).start()
    rcopy(half, half, s_ag.at[3], r_ag.at[3], sibling).wait_recv()

    def score(t, top):
        at = pl.multiple_of(t * 256, 256)
        part = nt(pall[pl.ds(at, 256), :], q_ref[...]) * SCALE
        st[pl.ds(at, 256), :] = part
        return jnp.maximum(top, jnp.max(part, axis=0, keepdims=True))

    top = lax.fori_loop(0, NP // 256, score, jnp.full((1, Q), NEG, F32))

    def hard(group, top):
        at = pl.multiple_of(group * PER * SLAB, PER * SLAB)
        row0 = pl.multiple_of(group * PER * CAP, PER * CAP)
        fs[...] = f[pl.ds(at, PER * SLAB), :].astype(F32)
        for c in range(C8):
            fn[pl.ds(row0, PER * CAP), c * 128:(c + 1) * 128] = fs[
                pl.ds(c, PER * CAP, stride=C8), :
            ].astype(BF16)
        part = nt(fn[pl.ds(row0, PER * CAP), :], q_ref[...]) * SCALE
        number = iota((PER * CAP, Q), 0) + row0
        taken = number == slots[0:1, :]
        for k in range(1, HARD):
            taken = taken | (number == slots[k:k + 1, :])
        part = jnp.where(taken, part, NEG)
        hs[pl.ds(row0, PER * CAP), :] = part
        return jnp.maximum(top, jnp.max(part, axis=0, keepdims=True))

    for group in range(GROUPS):
        n = PER - (1 if group == 0 else 0)
        ref = f.at[pl.ds(0, n * SLAB)]
        rcopy(ref, ref, s_row, r_row.at[group], sibling).wait_recv()
        top = hard(group, top)

    total = jnp.sum(jnp.exp(st[...] - top), axis=0, keepdims=True) + jnp.sum(
        jnp.exp(hs[...] - top), axis=0, keepdims=True
    )
    lse = top + jnp.log(total)

    p = pos_ref[...]
    answer_slot = (
        (((p >> 2) & 1) << 10)
        | (((p >> 7) & 3) << 8)
        | (((p >> 3) & 1) << 7)
        | (((p >> 9) & 3) << 5)
        | (((p >> 4) & 7) << 2)
        | (p & 3)
    )
    there = iota((256, 256), 0)
    source = (((there >> 2) & 7) << 5) | ((there >> 5) << 2) | (there & 3)
    swap = (iota((256, 256), 1) == source).astype(F32).astype(BF16)
    for t in range(NP // 256):
        rows = slice(t * 256, (t + 1) * 256)
        hit = (iota((256, Q), 0) + t * 256 == answer_slot).astype(F32)
        w = jnp.exp(st[rows, :] - lse) - hit
        st[rows, :] = w
        w = w.astype(BF16)
        wt[0, rows, :] = w
        wt[1, rows, :] = mm(swap, w).astype(BF16)

    def grads(j, side):
        def one(i, _):
            at = pl.multiple_of(side * 1024 + i * 256, 256)
            part = mm(wt[j // 2, pl.ds(at, 256), :], q_ref[:, j * 256:(j + 1) * 256])
            gpb[j, side, i] = part.reshape(8, 32, 256)
            return 0

        lax.fori_loop(0, NX, one, 0)

    for j in range(4):
        grads(j, 1 - core)
        rcopy(gpb.at[j, 1 - core], rc.at[j], s_rc.at[j], r_rc.at[j], sibling).start()
    for j in range(4):
        grads(j, core)

    def along(axis, i):
        return (
            device((x + i) % NX, y, z, core) if axis == "x"
            else device(x, (y + i) % NY, z, core) if axis == "y"
            else device(x, y, (z + i) % NZ, core)
        )

    where = {"x": x, "y": y, "z": z}
    size = {"x": NX, "y": NY, "z": NZ}

    for j in range(4):
        o, first_x = j // 2, j % 2 == 0
        a = "yz"[o]
        rcopy(gpb.at[j, 1 - core], rc.at[j], s_rc.at[j], r_rc.at[j], sibling).wait_recv()

        def add(i, _, j=j):
            gpb[j, core, i] = gpb[j, core, i] + rc[j, i]
            return 0

        lax.fori_loop(0, NX, add, 0)
        if first_x:
            for i in range(1, NX):
                rcopy(
                    gpb.at[j, core, (x + i) % NX], r1x.at[o, i - 1], s_1.at[j], r_1.at[j], along("x", i)
                ).start()
        else:
            for i in range(1, 8):
                rcopy(
                    gpb.at[j, core, :, (where[a] + i) % 8], r1a.at[o, i - 1], s_1.at[j], r_1.at[j], along(a, i)
                ).start()

    for half_at in range(2):
        cols = slice(half_at * 512, (half_at + 1) * 512)

        def passages(t, acc, cols=cols):
            at = pl.multiple_of(t * 256, 256)
            w = jnp.transpose(st[pl.ds(at, 256), :]).astype(BF16)
            return acc + mm(w, pall[pl.ds(at, 256), cols])

        def negatives(t, acc, cols=cols):
            at = pl.multiple_of(t * 256, 256)
            w = jnp.transpose(jnp.exp(hs[pl.ds(at, 256), :] - lse)).astype(BF16)
            return acc + mm(w, fn[pl.ds(at, 256), cols])

        acc = lax.fori_loop(0, NP // 256, passages, jnp.zeros((Q, 512), F32))
        acc = lax.fori_loop(0, SLOTS // 256, negatives, acc)
        gq_ref[:, cols] = acc * SCALE

    for j in range(4):
        o, first_x = j // 2, j % 2 == 0
        a = "yz"[o]
        if first_x:
            rcopy(r1x.at[o], r1x.at[o], s_1.at[j], r_1.at[j], sibling).wait_recv()
            acc = gpb[j, core, x]
            for i in range(NX - 1):
                acc = acc + r1x[o, i]
            ax[o] = acc
            for i in range(1, 8):
                rcopy(
                    ax.at[o, (where[a] + i) % 8], r2a.at[o, i - 1], s_2.at[j], r_2.at[j], along(a, i)
                ).start()
        else:
            rcopy(r1a.at[o], r1a.at[o], s_1.at[j], r_1.at[j], sibling).wait_recv()
            for i in range(NX):
                acc = gpb[j, core, i, where[a]]
                for n in range(7):
                    acc = acc + r1a[o, n, i]
                aa[o, i] = acc
            for i in range(1, NX):
                rcopy(
                    aa.at[o, (x + i) % NX], r2x.at[o, i - 1], s_2.at[j], r_2.at[j], along("x", i)
                ).start()

    for j in range(4):
        o, first_x = j // 2, j % 2 == 0
        a, b = "yz"[o], "zy"[o]
        if first_x:
            rcopy(r2a.at[o], r2a.at[o], s_2.at[j], r_2.at[j], sibling).wait_recv()
            acc = ax[o, where[a]]
            for i in range(7):
                acc = acc + r2a[o, i]
        else:
            rcopy(r2x.at[o], r2x.at[o], s_2.at[j], r_2.at[j], sibling).wait_recv()
            acc = aa[o, x]
            for i in range(NX - 1):
                acc = acc + r2x[o, i]
        for i in range(8):
            a3[j, i] = acc[i * 4:(i + 1) * 4, :]
        for i in range(1, 8):
            rcopy(
                a3.at[j, (where[b] + i) % 8], r3.at[j, i - 1], s_3.at[j], r_3.at[j], along(b, i)
            ).start()

    for j in range(4):
        b = "zy"[j // 2]
        rcopy(r3.at[j], r3.at[j], s_3.at[j], r_3.at[j], sibling).wait_recv()
        acc = a3[j, where[b]]
        for i in range(7):
            acc = acc + r3[j, i]
        gp_ref[:, j * 256:(j + 1) * 256] = acc * SCALE

    def left(ref, sem):
        rcopy(ref, ref, sem, sem, sibling).wait_send()

    left(reqin.at[pl.ds(0, NB - 1)], s_req)
    left(f.at[pl.ds(0, (NB - 1) * SLAB)], s_row)
    left(zbuf.at[pl.ds(0, NZ - 1)], s_ag.at[0])
    left(pall.at[pl.ds(0, 224)], s_ag.at[1])
    left(pall.at[pl.ds(0, 768)], s_ag.at[2])
    left(pall.at[pl.ds(0, 1024)], s_ag.at[3])
    for j in range(4):
        o, first_x = j // 2, j % 2 == 0
        left(rc.at[j], s_rc.at[j])
        left(r1x.at[o] if first_x else r1a.at[o], s_1.at[j])
        left(r2a.at[o] if first_x else r2x.at[o], s_2.at[j])
        left(r3.at[j], s_3.at[j])


def shards(queries, passages, negatives, neg_ids, positives):
    vmem = pl.BlockSpec(memory_space=pltpu.VMEM)
    dma = pltpu.SemaphoreType.DMA
    req, slots = pl.pallas_call(
        requests,
        out_shape=(
            jax.ShapeDtypeStruct((NB, 1, 128), I32),
            jax.ShapeDtypeStruct((128, Q), I32),
        ),
        in_specs=[vmem],
        out_specs=(vmem, vmem),
    )(neg_ids)
    return pl.pallas_call(
        kernel,
        out_shape=(
            jax.ShapeDtypeStruct((Q, D), F32),
            jax.ShapeDtypeStruct((4, D), F32),
        ),
        in_specs=[vmem] * 6,
        out_specs=(vmem, vmem),
        scratch_shapes=[
            pltpu.VMEM((NB, 1, 128), I32),
            pltpu.SMEM((NB, 1, 128), I32),
            pltpu.VMEM((ROWS, C8, 128), F32),
            pltpu.VMEM((NB * SLAB, 128), BF16),
            pltpu.VMEM((NB * SLAB, 128), BF16),
            pltpu.VMEM((PER * SLAB, 128), F32),
            pltpu.VMEM((SLOTS, D), BF16),
            pltpu.VMEM((NP, Q), F32),
            pltpu.VMEM((SLOTS, Q), F32),
            pltpu.VMEM((32, 128), F32),
            pltpu.VMEM((32, 128), BF16),
            pltpu.VMEM((NZ, 32, 128), BF16),
            pltpu.VMEM((NZ * 32, 128), F32),
            pltpu.VMEM((NP, D), BF16),
            pltpu.VMEM((2, NP, Q), BF16),
            pltpu.VMEM((4, 2, NX, 8, 32, 256), F32),
            pltpu.VMEM((4, NX, 8, 32, 256), F32),
            pltpu.VMEM((2, NX - 1, 8, 32, 256), F32),
            pltpu.VMEM((2, 7, NX, 32, 256), F32),
            pltpu.VMEM((2, 8, 32, 256), F32),
            pltpu.VMEM((2, NX, 32, 256), F32),
            pltpu.VMEM((2, NX - 1, 32, 256), F32),
            pltpu.VMEM((2, 7, 32, 256), F32),
            pltpu.VMEM((4, 8, 4, 256), F32),
            pltpu.VMEM((4, 7, 4, 256), F32),
            dma, dma, dma((4,)), dma, dma((GROUPS,)), dma((4,)),
            dma((4,)), dma((4,)), dma((4,)), dma((4,)),
            dma((4,)), dma((4,)), dma((4,)), dma((4,)), dma,
        ],
        compiler_params=pltpu.CompilerParams(
            collective_id=0, has_side_effects=True, vmem_limit_bytes=58 * 1024 * 1024
        ),
        cost_estimate=pl.CostEstimate(flops=4 * Q * NP * D * 2, bytes_accessed=1 << 24, transcendentals=0),
    )(req, slots, positives.reshape(1, Q), passages, queries, negatives)


def solution(mesh):
    rows = P(("blk", "grp"), None)
    return jax.shard_map(
        shards,
        mesh=mesh,
        in_specs=(rows, rows, rows, rows, P(("blk", "grp"))),
        out_specs=(rows, rows),
        check_vma=False,
    )
```

time: 2410 us -> 159 us (0.07)
  waiting for transfers between devices: 2150 us -> 0 us
  Pallas kernels: 0 us -> 151 us
  blocking collectives: 119 us -> 0 us
  local copies, waits for them, and re-layouts: 92.1 us -> 4.63 us
    unnamed x5 -> x0, waiting for transfers between devices: 1320 us -> none
    all_gather x2 -> x0, waiting for transfers between devices: 688 us -> none  [the longest x1 575 us: shards(): column = lax.all_gather(passages, 'blk', axis=0, tiled=True)]
    pallas_call x0 -> x2, Pallas kernels: none -> 151 us  [the longest x1 147 us: shards(): pl.pallas_call(kernel, out_shape=(jax.ShapeDtypeStruct((Q, D), F32), jax....]
    reduce_scatter x1 -> x0, waiting for transfers between devices: 144 us -> none  [shards(): lax.psum_scatter(jnp.dot(part_weights, column, preferred_element_type=jnp...]
    all_gather x3 -> x0, blocking collectives: 89.6 us -> none  [the longest x1 71.4 us: shards(): lax.all_gather(positives, 'grp', axis=0, tiled=True)]
    scatter x1 -> x0, local copies, waits for them, and re-layouts: 46.3 us -> none  [shards(): jnp.zeros((blk_size, capacity), jnp.int32).at[owners, ranks].set(local_rows)]
    gather x3 -> x0, local copies, waits for them, and re-layouts: 30 us -> none  [the longest x1 18.9 us: shards(): hard_rows = fetched[owners, ranks].reshape(q_count, hard_count, width)]
    all_to_all x1 -> x0, blocking collectives: 29.5 us -> none  [shards(): lax.all_to_all(requests, 'blk', split_axis=0, concat_axis=0, tiled=True)]
  transfers between devices with their start and end apart: 5 -> 0, of which waited for: 4 -> 0; matrix products, arithmetic and copies ran while one was open for 1% -> 0% of each run, Pallas kernels for 0% -> 0%
where the time goes in v1:
time: 159 us; the launch traced here: 156 us
  Pallas kernels  151 us (95%)
  local copies, waits for them, and re-layouts  4.63 us (3%)
    pallas_call x1, Pallas kernels, shards(): pl.pallas_call(kernel, out_shape=(jax.ShapeDtypeStruct((Q, D), F32), jax....  147 us
    unnamed x3, local copies, waits for them, and re-layouts  4.63 us
    pallas_call x1, Pallas kernels, shards(): pl.pallas_call(requests, out_shape=(jax.ShapeDtypeStruct((NB, 1, 128), I3...  3.38 us

profile of v1, /device:TPU:1, one launch (start us, length us, event | category | flops | bytes accessed | tf_op | source)
XLA Modules:
  0.0 156.0 jit_solution(15625475223227833956)
XLA Ops:
  0.6 1.4 copy.7.ids_ref
  2.1 3.4 %shard_map.68 = (s32[128,1,128]{2,1,0:T(1,128)}, s32[128,128]{1,0:T(8,128)}) custom-call(s32[128,7]{1,0:T(8,128)} %copy.7.ids_ref), custom_call_target="tpu_custom_call" | custom-call | tf_op jit(solution)/shard_map/pallas_call | solution.py:381
  5.4 147.4 %shard_map.69 = (f32[128,1024]{1,0:T(8,128)}, f32[4,1024]{1,0:T(4,128)}) custom-call(s32[128,1,128]{2,1,0:T(1,128)} %get-tuple-element.4.req, s32[128,128]{1,0:T(8,128)} %get-tuple-element.5.slots, s32[1,128]{1,0:T(1,128)} %bitcast.1, bf16[4,1024]{1,0:T(4,128)(2,1)} %pas_ref.1, bf16[128,1024]{1,0:T(8,128)(2,1)} %q_ref.1, bf16[896,1024]{1,0:T(8,128)(2,1)} %neg_ref.1), custom_call_target="tpu_custom_call" | custom-call | flops 2147483648 | bytes 16777216 | tf_op jit(solution)/shard_map/pallas_call | solution.py:390
  152.8 1.9 %copy.10 = f32[128,1024]{1,0:T(8,128)} copy(f32[128,1024]{1,0:T(8,128)} %get-tuple-element.8) | data formatting | bytes 1048576
  154.7 1.3 copy.11

commit v2 on v1

--- a/solution.py
+++ b/solution.py
@@ -50,7 +50,6 @@
 
 def requests(ids_ref, req, slots):
     mb = lax.axis_index("blk")
-    yl, x, z = mb // (NX * NZ), (mb // NZ) % NX, mb % NZ
 
     lane = iota((Q, 128), 1)
     lower = (iota((Q, Q), 0) > iota((Q, Q), 1)).astype(F32).astype(BF16)
@@ -63,11 +62,7 @@
         dev = jnp.floor((ids.astype(F32) + 0.5) * (1.0 / ROWS)).astype(I32)
         row = ids - dev * ROWS
         owner = dev >> 2
-        off = (
-            (((yl - (owner >> 5)) & 3) << 5)
-            | (((x - ((owner >> 3) & 3)) & 3) << 3)
-            | ((z - (owner & 7)) & 7)
-        )
+        off = owner ^ mb
         step = (off * INV) & (NB - 1)
         hot = (lane == step).astype(F32)
         rank = jnp.sum(hot * (mm(lower, hot.astype(BF16)) + base), axis=1, keepdims=True)
@@ -95,20 +90,15 @@
     yh, core = mg // 2, mg % 2
     y = yh * NYL + yl
 
-    def shifted(step, sign):
-        k = (step * MUL) % NB
-        ky, kx, kz = k // (NX * NZ), (k // NZ) % NX, k % NZ
-        py = (yl + NYL + sign * ky) % NYL
-        px = (x + NX + sign * kx) % NX
-        pz = (z + NZ + sign * kz) % NZ
-        return ((py * NX + px) * NZ + pz, mg)
+    def partner(step):
+        return (mb ^ ((step * MUL) & (NB - 1)), mg)
 
     sibling = device(x, y, z, 1 - core)
 
     barrier = pltpu.get_barrier_semaphore()
 
     def greet(step, _):
-        pl.semaphore_signal(barrier, inc=1, device_id=shifted(step, 1), device_id_type=MESH)
+        pl.semaphore_signal(barrier, inc=1, device_id=partner(step), device_id_type=MESH)
         return 0
 
     lax.fori_loop(1, NB, greet, 0)
@@ -126,7 +116,7 @@
     pl.semaphore_wait(barrier, NB - 1 + NYL + 1)
 
     def ask(step, _):
-        rcopy(req.at[step], reqin.at[step], s_req, r_req, shifted(step, -1)).start()
+        rcopy(req.at[step], reqin.at[step], s_req, r_req, partner(step)).start()
         return 0
 
     lax.fori_loop(1, NB, ask, 0)
@@ -168,7 +158,7 @@
         pick(step, g)
         at = pl.multiple_of(step * SLAB, 16)
         rcopy(
-            g.at[pl.ds(at, SLAB)], f.at[pl.ds(at, SLAB)], s_row, r_row.at[step // PER], shifted(step, 1)
+            g.at[pl.ds(at, SLAB)], f.at[pl.ds(at, SLAB)], s_row, r_row.at[step // PER], partner(step)
         ).start()
         return 0
 
@@ -176,14 +166,24 @@
     pick(0, f)
 
     rcopy(pall.at[pl.ds(0, 224)], pall.at[pl.ds(0, 224)], s_ag.at[1], r_ag.at[1], sibling).wait_recv()
-    for i in range(1, NX):
-        to = device((x + i) % NX, y, z, core)
-        block = pall.at[pl.ds(pl.multiple_of((core * NX + x) * 256, 256), 256)]
-        rcopy(block, block, s_ag.at[2], r_ag.at[2], to).start()
-    rcopy(pall.at[pl.ds(0, 768)], pall.at[pl.ds(0, 768)], s_ag.at[2], r_ag.at[2], sibling).wait_recv()
+    right, left_x = device((x + 1) % NX, y, z, core), device((x + NX - 1) % NX, y, z, core)
+
+    def slab(at, rows, extra=0):
+        return pall.at[pl.ds(pl.multiple_of((core * NX + at) * 256 + extra, 128), rows)]
+
+    for n, to in ((0, right), (1, left_x)):
+        rcopy(slab(x, 256), slab(x, 256), s_ag.at[2 + n], r_ag.at[2 + n], to).start()
+    for n, to in ((0, right), (1, left_x)):
+        came = (x + NX - 1) % NX if n == 0 else (x + 1) % NX
+        rcopy(slab(came, 256), slab(came, 256), s_ag.at[2 + n], r_ag.at[2 + n], to).wait_recv()
+        part = slab(came, 128, 128 * n)
+        rcopy(part, part, s_ag.at[4 + n], r_ag.at[4 + n], to).start()
+    for n in range(2):
+        part = slab((x + 2) % NX, 128, 128 * n)
+        rcopy(part, part, s_ag.at[4 + n], r_ag.at[4 + n], sibling).wait_recv()
     half = pall.at[pl.ds(pl.multiple_of(core * 1024, 1024), 1024)]
-    rcopy(half, half, s_ag.at[3], r_ag.at[3], sibling).start()
-    rcopy(half, half, s_ag.at[3], r_ag.at[3], sibling).wait_recv()
+    rcopy(half, half, s_ag.at[6], r_ag.at[6], sibling).start()
+    rcopy(half, half, s_ag.at[6], r_ag.at[6], sibling).wait_recv()
 
     def score(t, top):
         at = pl.multiple_of(t * 256, 256)
@@ -191,7 +191,16 @@
         st[pl.ds(at, 256), :] = part
         return jnp.maximum(top, jnp.max(part, axis=0, keepdims=True))
 
-    top = lax.fori_loop(0, NP // 256, score, jnp.full((1, Q), NEG, F32))
+    pool_top = lax.fori_loop(0, NP // 256, score, jnp.full((1, Q), NEG, F32))
+
+    def raise_(t, total):
+        at = pl.multiple_of(t * 256, 256)
+        part = jnp.exp(st[pl.ds(at, 256), :] - pool_top)
+        st[pl.ds(at, 256), :] = part
+        return total + jnp.sum(part, axis=0, keepdims=True)
+
+    pool_total = lax.fori_loop(0, NP // 256, raise_, jnp.zeros((1, Q), F32))
+    top = pool_top
 
     def hard(group, top):
         at = pl.multiple_of(group * PER * SLAB, PER * SLAB)
@@ -216,10 +225,9 @@
         rcopy(ref, ref, s_row, r_row.at[group], sibling).wait_recv()
         top = hard(group, top)
 
-    total = jnp.sum(jnp.exp(st[...] - top), axis=0, keepdims=True) + jnp.sum(
-        jnp.exp(hs[...] - top), axis=0, keepdims=True
-    )
+    total = pool_total * jnp.exp(pool_top - top) + jnp.sum(jnp.exp(hs[...] - top), axis=0, keepdims=True)
     lse = top + jnp.log(total)
+    factor = jnp.exp(pool_top - lse)
 
     p = pos_ref[...]
     answer_slot = (
@@ -233,14 +241,19 @@
     there = iota((256, 256), 0)
     source = (((there >> 2) & 7) << 5) | ((there >> 5) << 2) | (there & 3)
     swap = (iota((256, 256), 1) == source).astype(F32).astype(BF16)
-    for t in range(NP // 256):
-        rows = slice(t * 256, (t + 1) * 256)
-        hit = (iota((256, Q), 0) + t * 256 == answer_slot).astype(F32)
-        w = jnp.exp(st[rows, :] - lse) - hit
-        st[rows, :] = w
-        w = w.astype(BF16)
-        wt[0, rows, :] = w
-        wt[1, rows, :] = mm(swap, w).astype(BF16)
+
+    def weigh(side):
+        def one(i, _):
+            at = pl.multiple_of(side * 1024 + i * 256, 256)
+            hit = (iota((256, Q), 0) + at == answer_slot).astype(F32)
+            w = st[pl.ds(at, 256), :] * factor - hit
+            st[pl.ds(at, 256), :] = w
+            w = w.astype(BF16)
+            wt[0, pl.ds(at, 256), :] = w
+            wt[1, pl.ds(at, 256), :] = mm(swap, w).astype(BF16)
+            return 0
+
+        lax.fori_loop(0, NX, one, 0)
 
     def grads(j, side):
         def one(i, _):
@@ -251,25 +264,74 @@
 
         lax.fori_loop(0, NX, one, 0)
 
-    for j in range(4):
+    order = (1, 3, 0, 2)
+    weigh(1 - core)
+    for j in order:
         grads(j, 1 - core)
         rcopy(gpb.at[j, 1 - core], rc.at[j], s_rc.at[j], r_rc.at[j], sibling).start()
-    for j in range(4):
+    weigh(core)
+    for j in order:
         grads(j, core)
 
     def along(axis, i):
         return (
-            device((x + i) % NX, y, z, core) if axis == "x"
-            else device(x, (y + i) % NY, z, core) if axis == "y"
-            else device(x, y, (z + i) % NZ, core)
+            device((x + i + NX) % NX, y, z, core) if axis == "x"
+            else device(x, (y + i + NY) % NY, z, core) if axis == "y"
+            else device(x, y, (z + i + NZ) % NZ, core)
         )
 
     where = {"x": x, "y": y, "z": z}
-    size = {"x": NX, "y": NY, "z": NZ}
-
-    for j in range(4):
-        o, first_x = j // 2, j % 2 == 0
-        a = "yz"[o]
+
+    def ring(j):
+        axis = "xyxz"[j]
+        n = NX if axis == "x" else 8
+        o = j // 2
+
+        def own(half, target):
+            t = (where[axis] + target + n) % n
+            if axis == "x":
+                return gpb.at[j, core, t, pl.ds(half * 4, 4)]
+            return gpb.at[j, core, pl.ds(half * 2, 2), t]
+
+        def held(half, way, hop):
+            return (r1x if axis == "x" else r1a).at[o, half, way, hop]
+
+        def hops(half, way):
+            return n // 2 if half == way else n // 2 - 1
+
+        return axis, own, held, hops
+
+    def send(j, hop):
+        axis, own, held, hops = ring(j)
+        for half in range(2):
+            for way in range(2):
+                length, sign = hops(half, way), 1 - 2 * way
+                if hop >= length:
+                    continue
+                if hop == 0:
+                    source = own(half, sign * length)
+                else:
+                    source = held(half, way, hop - 1)
+                    rcopy(
+                        source, source, s_1.at[j, half, way, hop - 1], r_1.at[j, half, way, hop - 1], sibling
+                    ).wait_recv()
+                    source[...] = source[...] + own(half, sign * (length - hop))[...]
+                rcopy(
+                    source, held(half, way, hop), s_1.at[j, half, way, hop], r_1.at[j, half, way, hop],
+                    along(axis, sign),
+                ).start()
+
+    def arrived(j, half):
+        axis, own, held, hops = ring(j)
+        acc = own(half, 0)[...]
+        for way in range(2):
+            hop = hops(half, way) - 1
+            ref = held(half, way, hop)
+            rcopy(ref, ref, s_1.at[j, half, way, hop], r_1.at[j, half, way, hop], sibling).wait_recv()
+            acc = acc + ref[...]
+        return acc
+
+    for j in order:
         rcopy(gpb.at[j, 1 - core], rc.at[j], s_rc.at[j], r_rc.at[j], sibling).wait_recv()
 
         def add(i, _, j=j):
@@ -277,26 +339,17 @@
             return 0
 
         lax.fori_loop(0, NX, add, 0)
-        if first_x:
-            for i in range(1, NX):
-                rcopy(
-                    gpb.at[j, core, (x + i) % NX], r1x.at[o, i - 1], s_1.at[j], r_1.at[j], along("x", i)
-                ).start()
-        else:
-            for i in range(1, 8):
-                rcopy(
-                    gpb.at[j, core, :, (where[a] + i) % 8], r1a.at[o, i - 1], s_1.at[j], r_1.at[j], along(a, i)
-                ).start()
-
-    for half_at in range(2):
+        send(j, 0)
+
+    def queries_half(half_at):
         cols = slice(half_at * 512, (half_at + 1) * 512)
 
-        def passages(t, acc, cols=cols):
+        def passages(t, acc):
             at = pl.multiple_of(t * 256, 256)
             w = jnp.transpose(st[pl.ds(at, 256), :]).astype(BF16)
             return acc + mm(w, pall[pl.ds(at, 256), cols])
 
-        def negatives(t, acc, cols=cols):
+        def negatives(t, acc):
             at = pl.multiple_of(t * 256, 256)
             w = jnp.transpose(jnp.exp(hs[pl.ds(at, 256), :] - lse)).astype(BF16)
             return acc + mm(w, fn[pl.ds(at, 256), cols])
@@ -305,32 +358,33 @@
         acc = lax.fori_loop(0, SLOTS // 256, negatives, acc)
         gq_ref[:, cols] = acc * SCALE
 
-    for j in range(4):
-        o, first_x = j // 2, j % 2 == 0
+    queries_half(0)
+    for j in order:
+        send(j, 1)
+    queries_half(1)
+    for j in (1, 3):
+        send(j, 2)
+    for j in (0, 2):
+        o = j // 2
         a = "yz"[o]
-        if first_x:
-            rcopy(r1x.at[o], r1x.at[o], s_1.at[j], r_1.at[j], sibling).wait_recv()
-            acc = gpb[j, core, x]
-            for i in range(NX - 1):
-                acc = acc + r1x[o, i]
-            ax[o] = acc
-            for i in range(1, 8):
-                rcopy(
-                    ax.at[o, (where[a] + i) % 8], r2a.at[o, i - 1], s_2.at[j], r_2.at[j], along(a, i)
-                ).start()
-        else:
-            rcopy(r1a.at[o], r1a.at[o], s_1.at[j], r_1.at[j], sibling).wait_recv()
-            for i in range(NX):
-                acc = gpb[j, core, i, where[a]]
-                for n in range(7):
-                    acc = acc + r1a[o, n, i]
-                aa[o, i] = acc
-            for i in range(1, NX):
-                rcopy(
-                    aa.at[o, (x + i) % NX], r2x.at[o, i - 1], s_2.at[j], r_2.at[j], along("x", i)
-                ).start()
-
-    for j in range(4):
+        for half in range(2):
+            ax[o, pl.ds(half * 4, 4)] = arrived(j, half)
+        for i in range(1, 8):
+            rcopy(
+                ax.at[o, (where[a] + i) % 8], r2a.at[o, i - 1], s_2.at[j], r_2.at[j], along(a, i)
+            ).start()
+    for j in (1, 3):
+        send(j, 3)
+    for j in (1, 3):
+        o = j // 2
+        for half in range(2):
+            aa[o, pl.ds(half * 2, 2)] = arrived(j, half)
+        for i in range(1, NX):
+            rcopy(
+                aa.at[o, (x + i) % NX], r2x.at[o, i - 1], s_2.at[j], r_2.at[j], along("x", i)
+            ).start()
+
+    for j in (0, 2, 1, 3):
         o, first_x = j // 2, j % 2 == 0
         a, b = "yz"[o], "zy"[o]
         if first_x:
@@ -365,12 +419,18 @@
     left(f.at[pl.ds(0, (NB - 1) * SLAB)], s_row)
     left(zbuf.at[pl.ds(0, NZ - 1)], s_ag.at[0])
     left(pall.at[pl.ds(0, 224)], s_ag.at[1])
-    left(pall.at[pl.ds(0, 768)], s_ag.at[2])
-    left(pall.at[pl.ds(0, 1024)], s_ag.at[3])
+    for n in range(2):
+        left(pall.at[pl.ds(0, 256)], s_ag.at[2 + n])
+        left(pall.at[pl.ds(0, 128)], s_ag.at[4 + n])
+    left(pall.at[pl.ds(0, 1024)], s_ag.at[6])
     for j in range(4):
         o, first_x = j // 2, j % 2 == 0
         left(rc.at[j], s_rc.at[j])
-        left(r1x.at[o] if first_x else r1a.at[o], s_1.at[j])
+        _, _, held, hops = ring(j)
+        for half in range(2):
+            for way in range(2):
+                for hop in range(hops(half, way)):
+                    left(held(half, way, hop), s_1.at[j, half, way, hop])
         left(r2a.at[o] if first_x else r2x.at[o], s_2.at[j])
         left(r3.at[j], s_3.at[j])
 
@@ -413,16 +473,16 @@
             pltpu.VMEM((2, NP, Q), BF16),
             pltpu.VMEM((4, 2, NX, 8, 32, 256), F32),
             pltpu.VMEM((4, NX, 8, 32, 256), F32),
-            pltpu.VMEM((2, NX - 1, 8, 32, 256), F32),
-            pltpu.VMEM((2, 7, NX, 32, 256), F32),
+            pltpu.VMEM((2, 2, 2, 2, 4, 32, 256), F32),
+            pltpu.VMEM((2, 2, 2, 4, 2, 32, 256), F32),
             pltpu.VMEM((2, 8, 32, 256), F32),
             pltpu.VMEM((2, NX, 32, 256), F32),
             pltpu.VMEM((2, NX - 1, 32, 256), F32),
             pltpu.VMEM((2, 7, 32, 256), F32),
             pltpu.VMEM((4, 8, 4, 256), F32),
             pltpu.VMEM((4, 7, 4, 256), F32),
-            dma, dma, dma((4,)), dma, dma((GROUPS,)), dma((4,)),
-            dma((4,)), dma((4,)), dma((4,)), dma((4,)),
+            dma, dma, dma((7,)), dma, dma((GROUPS,)), dma((7,)),
+            dma((4,)), dma((4,)), dma((4, 2, 2, 4)), dma((4, 2, 2, 4)),
             dma((4,)), dma((4,)), dma((4,)), dma((4,)), dma,
         ],
         compiler_params=pltpu.CompilerParams(

time: 159 us -> 154 us (0.969)
  Pallas kernels: 151 us -> 146 us
    pallas_call x1, Pallas kernels: 147 us -> 143 us  [shards(): pl.pallas_call(kernel, out_shape=(jax.ShapeDtypeStruct((Q, D), F32), jax....]
where the time goes in v2:
time: 154 us; the launch traced here: 152 us
  Pallas kernels  146 us (95%)
  local copies, waits for them, and re-layouts  4.63 us (3%)
    pallas_call x1, Pallas kernels, shards(): pl.pallas_call(kernel, out_shape=(jax.ShapeDtypeStruct((Q, D), F32), jax....  143 us
    unnamed x3, local copies, waits for them, and re-layouts  4.63 us
    pallas_call x1, Pallas kernels, shards(): pl.pallas_call(requests, out_shape=(jax.ShapeDtypeStruct((NB, 1, 128), I3...  3.35 us

profile of v2, /device:TPU:1, one launch (start us, length us, event | category | flops | bytes accessed | tf_op | source)
XLA Modules:
  0.0 151.7 jit_solution(14337206470423228191)
XLA Ops:
  0.6 1.4 copy.7.ids_ref
  2.1 3.3 %shard_map.68 = (s32[128,1,128]{2,1,0:T(1,128)}, s32[128,128]{1,0:T(8,128)}) custom-call(s32[128,7]{1,0:T(8,128)} %copy.7.ids_ref), custom_call_target="tpu_custom_call" | custom-call | tf_op jit(solution)/shard_map/pallas_call | solution.py:441
  5.4 143.1 %shard_map.69 = (f32[128,1024]{1,0:T(8,128)}, f32[4,1024]{1,0:T(4,128)}) custom-call(s32[128,1,128]{2,1,0:T(1,128)} %get-tuple-element.4.req, s32[128,128]{1,0:T(8,128)} %get-tuple-element.5.slots, s32[1,128]{1,0:T(1,128)} %bitcast.1, bf16[4,1024]{1,0:T(4,128)(2,1)} %pas_ref.1, bf16[128,1024]{1,0:T(8,128)(2,1)} %q_ref.1, bf16[896,1024]{1,0:T(8,128)(2,1)} %neg_ref.1), custom_call_target="tpu_custom_call" | custom-call | flops 2147483648 | bytes 16777216 | tf_op jit(solution)/shard_map/pallas_call | solution.py:450
  148.5 1.9 %copy.10 = f32[128,1024]{1,0:T(8,128)} copy(f32[128,1024]{1,0:T(8,128)} %get-tuple-element.8) | data formatting | bytes 1048576
  150.4 1.3 copy.11

commit v3 on v2

--- a/solution.py
+++ b/solution.py
@@ -50,39 +50,41 @@
 
 def requests(ids_ref, req, slots):
     mb = lax.axis_index("blk")
-
-    lane = iota((Q, 128), 1)
-    lower = (iota((Q, Q), 0) > iota((Q, Q), 1)).astype(F32).astype(BF16)
-    base = jnp.zeros((1, 128), F32)
+    sub = iota((128, Q), 0)
+    before = (iota((Q, Q), 0) < iota((Q, Q), 1)).astype(F32).astype(BF16)
+    base = jnp.zeros((NB, 1), F32)
     want_hi = jnp.zeros((NB, 128), F32)
     want_lo = jnp.zeros((NB, 128), F32)
-    slot_cols = jnp.full((Q, 128), -1.0, F32)
+    slots[...] = jnp.full((8, Q), -1, I32)
     for k in range(HARD):
-        ids = ids_ref[:, k:k + 1]
+        ids = ids_ref[k:k + 1, :]
         dev = jnp.floor((ids.astype(F32) + 0.5) * (1.0 / ROWS)).astype(I32)
         row = ids - dev * ROWS
-        owner = dev >> 2
-        off = owner ^ mb
+        off = (dev >> 2) ^ mb
+        kz, kxy = off & (NZ - 1), off >> 3
         step = (off * INV) & (NB - 1)
-        hot = (lane == step).astype(F32)
-        rank = jnp.sum(hot * (mm(lower, hot.astype(BF16)) + base), axis=1, keepdims=True)
-        base = base + jnp.sum(hot, axis=0, keepdims=True)
-        slot_cols = jnp.where(lane == k, step.astype(F32) * CAP + rank, slot_cols)
-        at_rank = (lane.astype(F32) == rank).astype(F32)
-        hot_t = jnp.transpose(hot).astype(BF16)
-        want_hi = want_hi + mm(hot_t, (at_rank * (row >> 3).astype(F32)).astype(BF16))
-        want_lo = want_lo + mm(hot_t, (at_rank * (row & 7).astype(F32)).astype(BF16))
-    want = (want_hi * 8.0 + want_lo).astype(I32)
-    req[...] = want.reshape(NB, 1, 128)
-    slots[...] = jnp.transpose(slot_cols).astype(I32)
+        hot = (sub == kz * 16 + kxy).astype(F32)
+        hot16 = hot.astype(BF16)
+        rank = jnp.sum(hot * (mm(hot16, before) + base), axis=0, keepdims=True).astype(I32)
+        base = base + jnp.sum(hot, axis=1, keepdims=True)
+        slots[k:k + 1, :] = step * CAP + rank
+        at_lane = (sub == kz * 16 + rank).astype(F32)
+        want_hi = want_hi + nt(hot16, (at_lane * (row >> 3).astype(F32)).astype(BF16))
+        want_lo = want_lo + nt(hot16, (at_lane * (row & 7).astype(F32)).astype(BF16))
+    req[...] = (want_hi * 8.0 + want_lo).astype(I32).reshape(NZ, 16, 1, 128)
+
+
+def scaled(gq_in, gp_in, gq_ref, gp_ref):
+    gq_ref[...] = gq_in[...] * SCALE
+    gp_ref[...] = gp_in[...] * SCALE
 
 
 def kernel(
     req, slots, pos_ref, pas_ref, q_ref, neg_ref,
     gq_ref, gp_ref,
-    reqin, idsm, tab, g, f, fs, fn, st, hs, pst, pmine, zbuf, zf, pall,
+    asked, passed, reqin, idsm, tab, g, f, fs, fn, st, hs, pst, pmine, zbuf, zf, pall,
     wt, gpb, rc, r1x, r1a, ax, aa, r2x, r2a, a3, r3,
-    s_req, s_row, s_ag, r_req, r_row, r_ag, s_rc, r_rc, s_1, r_1, s_2, r_2, s_3, r_3, s_loc,
+    s_req, s_pass, s_y, s_row, s_ag, r_req, r_pass, r_y, r_row, r_ag, s_rc, r_rc, s_1, r_1, s_2, r_2, s_3, r_3, s_loc,
 ):
     mb = lax.axis_index("blk")
     mg = lax.axis_index("grp")
@@ -97,15 +99,16 @@
 
     barrier = pltpu.get_barrier_semaphore()
 
-    def greet(step, _):
-        pl.semaphore_signal(barrier, inc=1, device_id=partner(step), device_id_type=MESH)
-        return 0
-
-    lax.fori_loop(1, NB, greet, 0)
+    def greet(dev):
+        pl.semaphore_signal(barrier, inc=1, device_id=dev, device_id_type=MESH)
+
+    for i in range(1, NZ):
+        greet((mb ^ i, mg))
+    for n in range(1, 16):
+        greet((mb ^ (n * NZ), mg))
     for i in range(NYL):
-        other = device(x, (1 - yh) * NYL + i, z, core)
-        pl.semaphore_signal(barrier, inc=1, device_id=other, device_id_type=MESH)
-    pl.semaphore_signal(barrier, inc=1, device_id=sibling, device_id_type=MESH)
+        greet(device(x, (1 - yh) * NYL + i, z, core))
+    greet(sibling)
 
     for c in range(C8):
         pst[pl.ds(c, 4, stride=C8), :] = pas_ref[:, c * 128:(c + 1) * 128].astype(F32)
@@ -113,18 +116,24 @@
     pmine[...] = own
     zbuf[z] = own
 
-    pl.semaphore_wait(barrier, NB - 1 + NYL + 1)
-
-    def ask(step, _):
-        rcopy(req.at[step], reqin.at[step], s_req, r_req, partner(step)).start()
-        return 0
-
-    lax.fori_loop(1, NB, ask, 0)
-    reqin[0] = req[0]
+    pl.semaphore_wait(barrier, NZ - 1 + 15 + NYL + 1)
+
+    for i in range(1, NZ):
+        rcopy(req.at[i], asked.at[i], s_req, r_req, (mb ^ i, mg)).start()
+    asked[0] = req[0]
 
     for i in range(1, NZ):
         to = device(x, y, (z + i) % NZ, core)
         rcopy(pmine, zbuf.at[z], s_ag.at[0], r_ag.at[0], to).start()
+
+    rcopy(asked.at[pl.ds(0, NZ - 1)], asked.at[pl.ds(0, NZ - 1)], s_req, r_req, sibling).wait_recv()
+    total = asked[0]
+    for i in range(1, NZ):
+        total = total + asked[i]
+    passed[...] = total
+    for n in range(1, 16):
+        rcopy(passed.at[n], reqin.at[n], s_pass, r_pass, (mb ^ (n * NZ), mg)).start()
+    reqin[0] = passed[0]
 
     flat = tab.reshape(ROWS * C8, 128)
     for t in range(ROWS // 128):
@@ -138,20 +147,31 @@
     for c in range(C8):
         pall[pl.ds(mine, 32), c * 128:(c + 1) * 128] = zf[pl.ds(c, 32, stride=C8), :].astype(BF16)
 
-    for i in range(1, NY):
-        to = device(x, (y + i) % NY, z, core)
-        block = pall.at[pl.ds(mine, 32)]
-        rcopy(block, block, s_ag.at[1], r_ag.at[1], to).start()
-
-    rcopy(reqin.at[pl.ds(0, NB - 1)], reqin.at[pl.ds(0, NB - 1)], s_req, r_req, sibling).wait_recv()
+    def along_y(hop):
+        for n in range(2):
+            sign = 1 - 2 * n
+            rows = 16 if hop == 3 else 32
+            at = ((core * NX + x) * NY + (y + NY - sign * hop) % NY) * 32 + (16 * n if hop == 3 else 0)
+            block = pall.at[pl.ds(pl.multiple_of(at, 16), rows)]
+            if hop:
+                came = pall.at[pl.ds(0, 32)]
+                rcopy(came, came, s_y.at[n, hop - 1], r_y.at[n, hop - 1], sibling).wait_recv()
+            to = device(x, (y + NY + sign) % NY, z, core)
+            rcopy(block, block, s_y.at[n, hop], r_y.at[n, hop], to).start()
+
+    along_y(0)
+
+    rcopy(reqin.at[pl.ds(0, 15)], reqin.at[pl.ds(0, 15)], s_pass, r_pass, sibling).wait_recv()
     local = pltpu.make_async_copy(reqin, idsm, s_loc)
     local.start()
     local.wait()
 
     def pick(step, dst):
         at = pl.multiple_of(step * SLAB, 16)
+        k = (step * MUL) % NB
+        n, lane = k // NZ, (k % NZ) * 16
         for j in range(CAP // 2):
-            pair = jnp.concatenate([tab[idsm[step, 0, 2 * j]], tab[idsm[step, 0, 2 * j + 1]]], axis=0)
+            pair = jnp.concatenate([tab[idsm[n, 0, lane + 2 * j]], tab[idsm[n, 0, lane + 2 * j + 1]]], axis=0)
             dst[pl.ds(at + 16 * j, 16), :] = pair.astype(BF16)
 
     def answer(step, _):
@@ -162,10 +182,18 @@
         ).start()
         return 0
 
-    lax.fori_loop(1, NB, answer, 0)
+    lax.fori_loop(1, 16, answer, 0)
+    along_y(1)
+    lax.fori_loop(16, 32, answer, 0)
+    along_y(2)
+    lax.fori_loop(32, 48, answer, 0)
+    along_y(3)
+    lax.fori_loop(48, NB, answer, 0)
     pick(0, f)
 
-    rcopy(pall.at[pl.ds(0, 224)], pall.at[pl.ds(0, 224)], s_ag.at[1], r_ag.at[1], sibling).wait_recv()
+    for n in range(2):
+        came = pall.at[pl.ds(0, 16)]
+        rcopy(came, came, s_y.at[n, 3], r_y.at[n, 3], sibling).wait_recv()
     right, left_x = device((x + 1) % NX, y, z, core), device((x + NX - 1) % NX, y, z, core)
 
     def slab(at, rows, extra=0):
@@ -356,7 +384,7 @@
 
         acc = lax.fori_loop(0, NP // 256, passages, jnp.zeros((Q, 512), F32))
         acc = lax.fori_loop(0, SLOTS // 256, negatives, acc)
-        gq_ref[:, cols] = acc * SCALE
+        gq_ref[:, cols] = acc
 
     queries_half(0)
     for j in order:
@@ -410,15 +438,18 @@
         acc = a3[j, where[b]]
         for i in range(7):
             acc = acc + r3[j, i]
-        gp_ref[:, j * 256:(j + 1) * 256] = acc * SCALE
+        gp_ref[:, j * 256:(j + 1) * 256] = acc
 
     def left(ref, sem):
         rcopy(ref, ref, sem, sem, sibling).wait_send()
 
-    left(reqin.at[pl.ds(0, NB - 1)], s_req)
+    left(asked.at[pl.ds(0, NZ - 1)], s_req)
+    left(reqin.at[pl.ds(0, 15)], s_pass)
     left(f.at[pl.ds(0, (NB - 1) * SLAB)], s_row)
     left(zbuf.at[pl.ds(0, NZ - 1)], s_ag.at[0])
-    left(pall.at[pl.ds(0, 224)], s_ag.at[1])
+    for n in range(2):
+        for hop in range(4):
+            left(pall.at[pl.ds(0, 16 if hop == 3 else 32)], s_y.at[n, hop])
     for n in range(2):
         left(pall.at[pl.ds(0, 256)], s_ag.at[2 + n])
         left(pall.at[pl.ds(0, 128)], s_ag.at[4 + n])
@@ -441,13 +472,13 @@
     req, slots = pl.pallas_call(
         requests,
         out_shape=(
-            jax.ShapeDtypeStruct((NB, 1, 128), I32),
-            jax.ShapeDtypeStruct((128, Q), I32),
+            jax.ShapeDtypeStruct((NZ, 16, 1, 128), I32),
+            jax.ShapeDtypeStruct((8, Q), I32),
         ),
         in_specs=[vmem],
         out_specs=(vmem, vmem),
-    )(neg_ids)
-    return pl.pallas_call(
+    )(neg_ids.T)
+    sums = pl.pallas_call(
         kernel,
         out_shape=(
             jax.ShapeDtypeStruct((Q, D), F32),
@@ -456,8 +487,10 @@
         in_specs=[vmem] * 6,
         out_specs=(vmem, vmem),
         scratch_shapes=[
-            pltpu.VMEM((NB, 1, 128), I32),
-            pltpu.SMEM((NB, 1, 128), I32),
+            pltpu.VMEM((NZ, 16, 1, 128), I32),
+            pltpu.VMEM((16, 1, 128), I32),
+            pltpu.VMEM((16, 1, 128), I32),
+            pltpu.SMEM((16, 1, 128), I32),
             pltpu.VMEM((ROWS, C8, 128), F32),
             pltpu.VMEM((NB * SLAB, 128), BF16),
             pltpu.VMEM((NB * SLAB, 128), BF16),
@@ -481,7 +514,7 @@
             pltpu.VMEM((2, 7, 32, 256), F32),
             pltpu.VMEM((4, 8, 4, 256), F32),
             pltpu.VMEM((4, 7, 4, 256), F32),
-            dma, dma, dma((7,)), dma, dma((GROUPS,)), dma((7,)),
+            dma, dma, dma((2, 4)), dma, dma((7,)), dma, dma, dma((2, 4)), dma((GROUPS,)), dma((7,)),
             dma((4,)), dma((4,)), dma((4, 2, 2, 4)), dma((4, 2, 2, 4)),
             dma((4,)), dma((4,)), dma((4,)), dma((4,)), dma,
         ],
@@ -490,6 +523,15 @@
         ),
         cost_estimate=pl.CostEstimate(flops=4 * Q * NP * D * 2, bytes_accessed=1 << 24, transcendentals=0),
     )(req, slots, positives.reshape(1, Q), passages, queries, negatives)
+    return pl.pallas_call(
+        scaled,
+        out_shape=(
+            jax.ShapeDtypeStruct((Q, D), F32),
+            jax.ShapeDtypeStruct((4, D), F32),
+        ),
+        in_specs=[vmem] * 2,
+        out_specs=(vmem, vmem),
+    )(*sums)
 
 
 def solution(mesh):

time: 154 us -> 153 us (level); the launches traced: 152 us -> 153 us
  Pallas kernels: 146 us -> 152 us
  local copies, waits for them, and re-layouts: 4.63 us -> 0 us
    unnamed x3 -> x0, local copies, waits for them, and re-layouts: 4.63 us -> none
    pallas_call x1, Pallas kernels: 143 us -> 147 us  [shards(): pl.pallas_call(kernel, out_shape=(jax.ShapeDtypeStruct((Q, D), F32), jax....]
    pallas_call x1 -> x2, Pallas kernels: 3.35 us -> 4.66 us  [the longest x1 2.78 us: shards(): pl.pallas_call(requests, out_shape=(jax.ShapeDtypeStruct((NZ, 16, 1, 128)...]
where the time goes in v3:
time: 153 us
  Pallas kernels  152 us (99%)
    pallas_call x1, Pallas kernels, shards(): pl.pallas_call(kernel, out_shape=(jax.ShapeDtypeStruct((Q, D), F32), jax....  147 us

profile of v3, /device:TPU:1, one launch (start us, length us, event | category | flops | bytes accessed | tf_op | source)
XLA Modules:
  0.0 152.5 jit_solution(2612780447356162620)
XLA Ops:
  0.6 2.8 %shard_map.68 = (s32[8,16,1,128]{3,2,1,0:T(1,128)}, s32[8,128]{1,0:T(8,128)}) custom-call(s32[7,128]{1,0:T(8,128)} %bitcast.2), custom_call_target="tpu_custom_call" | custom-call | tf_op jit(solution)/shard_map/pallas_call | solution.py:472
  3.4 147.2 %shard_map.69 = (f32[128,1024]{1,0:T(8,128)}, f32[4,1024]{1,0:T(4,128)}) custom-call(s32[8,16,1,128]{3,2,1,0:T(1,128)} %get-tuple-element.6.req, s32[8,128]{1,0:T(8,128)} %get-tuple-element.7.slots, s32[1,128]{1,0:T(1,128)} %bitcast.3, bf16[4,1024]{1,0:T(4,128)(2,1)} %pas_ref.1, bf16[128,1024]{1,0:T(8,128)(2,1)} %q_ref.1, bf16[896,1024]{1,0:T(8,128)(2,1)} %neg_ref.1), custom_call_target="tpu_custom_call" | custom-call | flops 2147483648 | bytes 16777216 | tf_op jit(solution)/shard_map/pallas_call | solution.py:481
  150.7 1.9 %shard_map.70 = (f32[128,1024]{1,0:T(8,128)}, f32[4,1024]{1,0:T(4,128)}) custom-call(f32[128,1024]{1,0:T(8,128)} %get-tuple-element.8.gq_in, f32[4,1024]{1,0:T(4,128)} %get-tuple-element.9.gp_in), custom_call_target="tpu_custom_call" | custom-call | tf_op jit(solution)/shard_map/pallas_call | solution.py:526

commit v4 on v3

--- a/solution.py
+++ b/solution.py
@@ -20,6 +20,8 @@
 SLAB = CAP * C8
 GROUPS = 8
 PER = NB // GROUPS
+CHUNKS = 16
+STEPS = NB // CHUNKS
 SLOTS = NB * CAP
 NP = 2048
 SCALE = 3.0 / math.sqrt(D)
@@ -178,40 +180,45 @@
         pick(step, g)
         at = pl.multiple_of(step * SLAB, 16)
         rcopy(
-            g.at[pl.ds(at, SLAB)], f.at[pl.ds(at, SLAB)], s_row, r_row.at[step // PER], partner(step)
+            g.at[pl.ds(at, SLAB)], f.at[pl.ds(at, SLAB)], s_row.at[step // STEPS], r_row.at[step // PER], partner(step)
         ).start()
         return 0
 
-    lax.fori_loop(1, 16, answer, 0)
-    along_y(1)
-    lax.fori_loop(16, 32, answer, 0)
-    along_y(2)
-    lax.fori_loop(32, 48, answer, 0)
-    along_y(3)
-    lax.fori_loop(48, NB, answer, 0)
-    pick(0, f)
-
-    for n in range(2):
-        came = pall.at[pl.ds(0, 16)]
-        rcopy(came, came, s_y.at[n, 3], r_y.at[n, 3], sibling).wait_recv()
+    def gone(chunk):
+        ref = f.at[pl.ds(0, (STEPS - (1 if chunk == 0 else 0)) * SLAB)]
+        rcopy(ref, ref, s_row.at[chunk], s_row.at[chunk], sibling).wait_send()
+
+    def answers(chunk):
+        lax.fori_loop(max(1, chunk * STEPS), (chunk + 1) * STEPS, answer, 0)
+        if chunk >= 2:
+            gone(chunk - 2)
+
     right, left_x = device((x + 1) % NX, y, z, core), device((x + NX - 1) % NX, y, z, core)
 
     def slab(at, rows, extra=0):
         return pall.at[pl.ds(pl.multiple_of((core * NX + at) * 256 + extra, 128), rows)]
 
-    for n, to in ((0, right), (1, left_x)):
-        rcopy(slab(x, 256), slab(x, 256), s_ag.at[2 + n], r_ag.at[2 + n], to).start()
-    for n, to in ((0, right), (1, left_x)):
-        came = (x + NX - 1) % NX if n == 0 else (x + 1) % NX
-        rcopy(slab(came, 256), slab(came, 256), s_ag.at[2 + n], r_ag.at[2 + n], to).wait_recv()
-        part = slab(came, 128, 128 * n)
-        rcopy(part, part, s_ag.at[4 + n], r_ag.at[4 + n], to).start()
-    for n in range(2):
-        part = slab((x + 2) % NX, 128, 128 * n)
-        rcopy(part, part, s_ag.at[4 + n], r_ag.at[4 + n], sibling).wait_recv()
+    def along_x(hop):
+        for n, to in ((0, right), (1, left_x)):
+            if hop == 0:
+                came = pall.at[pl.ds(0, 16)]
+                rcopy(came, came, s_y.at[n, 3], r_y.at[n, 3], sibling).wait_recv()
+        for n, to in ((0, right), (1, left_x)):
+            if hop == 0:
+                rcopy(slab(x, 256), slab(x, 256), s_ag.at[2 + n], r_ag.at[2 + n], to).start()
+            else:
+                came = (x + NX - 1) % NX if n == 0 else (x + 1) % NX
+                rcopy(slab(came, 256), slab(came, 256), s_ag.at[2 + n], r_ag.at[2 + n], to).wait_recv()
+                part = slab(came, 128, 128 * n)
+                rcopy(part, part, s_ag.at[4 + n], r_ag.at[4 + n], to).start()
+
     half = pall.at[pl.ds(pl.multiple_of(core * 1024, 1024), 1024)]
-    rcopy(half, half, s_ag.at[6], r_ag.at[6], sibling).start()
-    rcopy(half, half, s_ag.at[6], r_ag.at[6], sibling).wait_recv()
+
+    def across():
+        for n in range(2):
+            part = slab((x + 2) % NX, 128, 128 * n)
+            rcopy(part, part, s_ag.at[4 + n], r_ag.at[4 + n], sibling).wait_recv()
+        rcopy(half, half, s_ag.at[6], r_ag.at[6], sibling).start()
 
     def score(t, top):
         at = pl.multiple_of(t * 256, 256)
@@ -219,16 +226,17 @@
         st[pl.ds(at, 256), :] = part
         return jnp.maximum(top, jnp.max(part, axis=0, keepdims=True))
 
-    pool_top = lax.fori_loop(0, NP // 256, score, jnp.full((1, Q), NEG, F32))
-
-    def raise_(t, total):
+    def raise_(t, carry):
+        pool_top, total = carry
         at = pl.multiple_of(t * 256, 256)
         part = jnp.exp(st[pl.ds(at, 256), :] - pool_top)
         st[pl.ds(at, 256), :] = part
-        return total + jnp.sum(part, axis=0, keepdims=True)
-
-    pool_total = lax.fori_loop(0, NP // 256, raise_, jnp.zeros((1, Q), F32))
-    top = pool_top
+        return pool_top, total + jnp.sum(part, axis=0, keepdims=True)
+
+    def pool():
+        rcopy(half, half, s_ag.at[6], r_ag.at[6], sibling).wait_recv()
+        pool_top = lax.fori_loop(0, NP // 256, score, jnp.full((1, Q), NEG, F32))
+        return lax.fori_loop(0, NP // 256, raise_, (pool_top, jnp.zeros((1, Q), F32)))
 
     def hard(group, top):
         at = pl.multiple_of(group * PER * SLAB, PER * SLAB)
@@ -247,11 +255,34 @@
         hs[pl.ds(row0, PER * CAP), :] = part
         return jnp.maximum(top, jnp.max(part, axis=0, keepdims=True))
 
-    for group in range(GROUPS):
+    def group_in(group, top):
         n = PER - (1 if group == 0 else 0)
         ref = f.at[pl.ds(0, n * SLAB)]
-        rcopy(ref, ref, s_row, r_row.at[group], sibling).wait_recv()
-        top = hard(group, top)
+        rcopy(ref, ref, s_pass, r_row.at[group], sibling).wait_recv()
+        return hard(group, top)
+
+    hard_top = jnp.full((1, Q), NEG, F32)
+    along_y(1)
+    for chunk in range(CHUNKS):
+        answers(chunk)
+        if chunk == 0:
+            pick(0, f)
+            along_y(2)
+        elif chunk == 1:
+            along_y(3)
+        elif chunk == 2:
+            along_x(0)
+        elif chunk == 5:
+            along_x(1)
+        elif chunk == 7:
+            across()
+        elif chunk == 10:
+            pool_top, pool_total = pool()
+        if chunk >= 5 and chunk % 2 == 1:
+            hard_top = group_in((chunk - 5) // 2, hard_top)
+    for group in range((CHUNKS - 4) // 2, GROUPS):
+        hard_top = group_in(group, hard_top)
+    top = jnp.maximum(pool_top, hard_top)
 
     total = pool_total * jnp.exp(pool_top - top) + jnp.sum(jnp.exp(hs[...] - top), axis=0, keepdims=True)
     lse = top + jnp.log(total)
@@ -298,8 +329,7 @@
         grads(j, 1 - core)
         rcopy(gpb.at[j, 1 - core], rc.at[j], s_rc.at[j], r_rc.at[j], sibling).start()
     weigh(core)
-    for j in order:
-        grads(j, core)
+    grads(order[0], core)
 
     def along(axis, i):
         return (
@@ -359,7 +389,9 @@
             acc = acc + ref[...]
         return acc
 
-    for j in order:
+    for place, j in enumerate(order):
+        if place:
+            grads(j, core)
         rcopy(gpb.at[j, 1 - core], rc.at[j], s_rc.at[j], r_rc.at[j], sibling).wait_recv()
 
         def add(i, _, j=j):
@@ -445,7 +477,8 @@
 
     left(asked.at[pl.ds(0, NZ - 1)], s_req)
     left(reqin.at[pl.ds(0, 15)], s_pass)
-    left(f.at[pl.ds(0, (NB - 1) * SLAB)], s_row)
+    gone(CHUNKS - 2)
+    gone(CHUNKS - 1)
     left(zbuf.at[pl.ds(0, NZ - 1)], s_ag.at[0])
     for n in range(2):
         for hop in range(4):
@@ -514,7 +547,7 @@
             pltpu.VMEM((2, 7, 32, 256), F32),
             pltpu.VMEM((4, 8, 4, 256), F32),
             pltpu.VMEM((4, 7, 4, 256), F32),
-            dma, dma, dma((2, 4)), dma, dma((7,)), dma, dma, dma((2, 4)), dma((GROUPS,)), dma((7,)),
+            dma, dma, dma((2, 4)), dma((CHUNKS,)), dma((7,)), dma, dma, dma((2, 4)), dma((GROUPS,)), dma((7,)),
             dma((4,)), dma((4,)), dma((4, 2, 2, 4)), dma((4, 2, 2, 4)),
             dma((4,)), dma((4,)), dma((4,)), dma((4,)), dma,
         ],

time: 153 us -> 151 us (0.987)
  Pallas kernels: 152 us -> 149 us
    pallas_call x1, Pallas kernels: 147 us -> 144 us  [shards(): pl.pallas_call(kernel, out_shape=(jax.ShapeDtypeStruct((Q, D), F32), jax....]
where the time goes in v4:
time: 151 us; the launch traced here: 149 us
  Pallas kernels  149 us (99%)
    pallas_call x1, Pallas kernels, shards(): pl.pallas_call(kernel, out_shape=(jax.ShapeDtypeStruct((Q, D), F32), jax....  144 us

profile of v4, /device:TPU:1, one launch (start us, length us, event | category | flops | bytes accessed | tf_op | source)
XLA Modules:
  0.0 149.4 jit_solution(17400849825901203641)
XLA Ops:
  0.6 2.8 %shard_map.68 = (s32[8,16,1,128]{3,2,1,0:T(1,128)}, s32[8,128]{1,0:T(8,128)}) custom-call(s32[7,128]{1,0:T(8,128)} %bitcast.2), custom_call_target="tpu_custom_call" | custom-call | tf_op jit(solution)/shard_map/pallas_call | solution.py:505
  3.4 144.1 %shard_map.69 = (f32[128,1024]{1,0:T(8,128)}, f32[4,1024]{1,0:T(4,128)}) custom-call(s32[8,16,1,128]{3,2,1,0:T(1,128)} %get-tuple-element.6.req, s32[8,128]{1,0:T(8,128)} %get-tuple-element.7.slots, s32[1,128]{1,0:T(1,128)} %bitcast.3, bf16[4,1024]{1,0:T(4,128)(2,1)} %pas_ref.1, bf16[128,1024]{1,0:T(8,128)(2,1)} %q_ref.1, bf16[896,1024]{1,0:T(8,128)(2,1)} %neg_ref.1), custom_call_target="tpu_custom_call" | custom-call | flops 2147483648 | bytes 16777216 | tf_op jit(solution)/shard_map/pallas_call | solution.py:514
  147.5 1.9 %shard_map.70 = (f32[128,1024]{1,0:T(8,128)}, f32[4,1024]{1,0:T(4,128)}) custom-call(f32[128,1024]{1,0:T(8,128)} %get-tuple-element.8.gq_in, f32[4,1024]{1,0:T(4,128)} %get-tuple-element.9.gp_in), custom_call_target="tpu_custom_call" | custom-call | tf_op jit(solution)/shard_map/pallas_call | solution.py:559

commit v5 on v4

--- a/solution.py
+++ b/solution.py
@@ -22,6 +22,7 @@
 PER = NB // GROUPS
 CHUNKS = 16
 STEPS = NB // CHUNKS
+VIA = 12
 SLOTS = NB * CAP
 NP = 2048
 SCALE = 3.0 / math.sqrt(D)
@@ -85,8 +86,8 @@
     req, slots, pos_ref, pas_ref, q_ref, neg_ref,
     gq_ref, gp_ref,
     asked, passed, reqin, idsm, tab, g, f, fs, fn, st, hs, pst, pmine, zbuf, zf, pall,
-    wt, gpb, rc, r1x, r1a, ax, aa, r2x, r2a, a3, r3,
-    s_req, s_pass, s_y, s_row, s_ag, r_req, r_pass, r_y, r_row, r_ag, s_rc, r_rc, s_1, r_1, s_2, r_2, s_3, r_3, s_loc,
+    gv, hv, wt, gpb, rc, r1x, r1a, ax, aa, r2x, r2a, a3, r3,
+    s_req, s_pass, s_y, s_row, s_ag, r_req, r_pass, r_y, r_row, r_ag, s_rc, r_rc, s_1, r_1, s_2, r_2, s_3, r_3, s_loc, s_via, r_via,
 ):
     mb = lax.axis_index("blk")
     mg = lax.axis_index("grp")
@@ -168,8 +169,7 @@
     local.start()
     local.wait()
 
-    def pick(step, dst):
-        at = pl.multiple_of(step * SLAB, 16)
+    def pick(step, dst, at):
         k = (step * MUL) % NB
         n, lane = k // NZ, (k % NZ) * 16
         for j in range(CAP // 2):
@@ -177,19 +177,36 @@
             dst[pl.ds(at + 16 * j, 16), :] = pair.astype(BF16)
 
     def answer(step, _):
-        pick(step, g)
         at = pl.multiple_of(step * SLAB, 16)
+        pick(step, g, at)
         rcopy(
             g.at[pl.ds(at, SLAB)], f.at[pl.ds(at, SLAB)], s_row.at[step // STEPS], r_row.at[step // PER], partner(step)
         ).start()
         return 0
 
+    def gather_via(u, _):
+        pick(u * PER + VIA, gv, pl.multiple_of(u * SLAB, 16))
+        return 0
+
+    def pass_on(u, _):
+        step = u * PER + VIA
+        source = mb - z + (z + 1) % NZ
+        to = (source ^ ((step * MUL) & (NB - 1)), mg)
+        block = hv.at[pl.ds(pl.multiple_of(u * SLAB, 16), SLAB)]
+        at = pl.multiple_of(step * SLAB, 16)
+        rcopy(block, f.at[pl.ds(at, SLAB)], s_via.at[1], r_row.at[u], to).start()
+        return 0
+
     def gone(chunk):
-        ref = f.at[pl.ds(0, (STEPS - (1 if chunk == 0 else 0)) * SLAB)]
+        ref = f.at[pl.ds(0, (STEPS - (1 if chunk == 0 or chunk % 2 else 0)) * SLAB)]
         rcopy(ref, ref, s_row.at[chunk], s_row.at[chunk], sibling).wait_send()
 
     def answers(chunk):
-        lax.fori_loop(max(1, chunk * STEPS), (chunk + 1) * STEPS, answer, 0)
+        first, last = max(1, chunk * STEPS), (chunk + 1) * STEPS
+        if chunk % 2:
+            lax.fori_loop(first, chunk // 2 * PER + VIA, answer, 0)
+            first = chunk // 2 * PER + VIA + 1
+        lax.fori_loop(first, last, answer, 0)
         if chunk >= 2:
             gone(chunk - 2)
 
@@ -262,15 +279,19 @@
         return hard(group, top)
 
     hard_top = jnp.full((1, Q), NEG, F32)
+    lax.fori_loop(0, GROUPS, gather_via, 0)
+    rcopy(gv, hv, s_via.at[0], r_via, device(x, y, (z + NZ - 1) % NZ, core)).start()
     along_y(1)
     for chunk in range(CHUNKS):
         answers(chunk)
         if chunk == 0:
-            pick(0, f)
+            pick(0, f, 0)
             along_y(2)
         elif chunk == 1:
             along_y(3)
         elif chunk == 2:
+            rcopy(gv, hv, s_via.at[0], r_via, sibling).wait_recv()
+            lax.fori_loop(0, GROUPS, pass_on, 0)
             along_x(0)
         elif chunk == 5:
             along_x(1)
@@ -323,7 +344,7 @@
 
         lax.fori_loop(0, NX, one, 0)
 
-    order = (1, 3, 0, 2)
+    order = (0, 1, 3, 2)
     weigh(1 - core)
     for j in order:
         grads(j, 1 - core)
@@ -361,23 +382,22 @@
 
     def send(j, hop):
         axis, own, held, hops = ring(j)
-        for half in range(2):
-            for way in range(2):
-                length, sign = hops(half, way), 1 - 2 * way
-                if hop >= length:
-                    continue
-                if hop == 0:
-                    source = own(half, sign * length)
-                else:
-                    source = held(half, way, hop - 1)
-                    rcopy(
-                        source, source, s_1.at[j, half, way, hop - 1], r_1.at[j, half, way, hop - 1], sibling
-                    ).wait_recv()
-                    source[...] = source[...] + own(half, sign * (length - hop))[...]
+        for half, way in ((0, 0), (1, 1), (1, 0), (0, 1)):
+            length, sign = hops(half, way), 1 - 2 * way
+            if hop >= length:
+                continue
+            if hop == 0:
+                source = own(half, sign * length)
+            else:
+                source = held(half, way, hop - 1)
                 rcopy(
-                    source, held(half, way, hop), s_1.at[j, half, way, hop], r_1.at[j, half, way, hop],
-                    along(axis, sign),
-                ).start()
+                    source, source, s_1.at[j, half, way, hop - 1], r_1.at[j, half, way, hop - 1], sibling
+                ).wait_recv()
+                source[...] = source[...] + own(half, sign * (length - hop))[...]
+            rcopy(
+                source, held(half, way, hop), s_1.at[j, half, way, hop], r_1.at[j, half, way, hop],
+                along(axis, sign),
+            ).start()
 
     def arrived(j, half):
         axis, own, held, hops = ring(j)
@@ -422,27 +442,32 @@
     for j in order:
         send(j, 1)
     queries_half(1)
-    for j in (1, 3):
-        send(j, 2)
-    for j in (0, 2):
-        o = j // 2
-        a = "yz"[o]
-        for half in range(2):
-            ax[o, pl.ds(half * 4, 4)] = arrived(j, half)
-        for i in range(1, 8):
-            rcopy(
-                ax.at[o, (where[a] + i) % 8], r2a.at[o, i - 1], s_2.at[j], r_2.at[j], along(a, i)
-            ).start()
-    for j in (1, 3):
-        send(j, 3)
-    for j in (1, 3):
-        o = j // 2
-        for half in range(2):
-            aa[o, pl.ds(half * 2, 2)] = arrived(j, half)
-        for i in range(1, NX):
-            rcopy(
-                aa.at[o, (x + i) % NX], r2x.at[o, i - 1], s_2.at[j], r_2.at[j], along("x", i)
-            ).start()
+    def second(j):
+        axis, o = "xyxz"[j], j // 2
+        if axis == "x":
+            a = "yz"[o]
+            for half in range(2):
+                ax[o, pl.ds(half * 4, 4)] = arrived(j, half)
+            for i in range(1, 8):
+                rcopy(
+                    ax.at[o, (where[a] + i) % 8], r2a.at[o, i - 1], s_2.at[j], r_2.at[j], along(a, i)
+                ).start()
+        else:
+            for half in range(2):
+                aa[o, pl.ds(half * 2, 2)] = arrived(j, half)
+            for i in range(1, NX):
+                rcopy(
+                    aa.at[o, (x + i) % NX], r2x.at[o, i - 1], s_2.at[j], r_2.at[j], along("x", i)
+                ).start()
+
+    send(1, 2)
+    send(3, 2)
+    second(0)
+    send(1, 3)
+    send(3, 3)
+    second(2)
+    second(1)
+    second(3)
 
     for j in (0, 2, 1, 3):
         o, first_x = j // 2, j % 2 == 0
@@ -477,6 +502,8 @@
 
     left(asked.at[pl.ds(0, NZ - 1)], s_req)
     left(reqin.at[pl.ds(0, 15)], s_pass)
+    left(hv, s_via.at[0])
+    left(hv, s_via.at[1])
     gone(CHUNKS - 2)
     gone(CHUNKS - 1)
     left(zbuf.at[pl.ds(0, NZ - 1)], s_ag.at[0])
@@ -536,6 +563,8 @@
             pltpu.VMEM((NZ, 32, 128), BF16),
             pltpu.VMEM((NZ * 32, 128), F32),
             pltpu.VMEM((NP, D), BF16),
+            pltpu.VMEM((GROUPS * SLAB, 128), BF16),
+            pltpu.VMEM((GROUPS * SLAB, 128), BF16),
             pltpu.VMEM((2, NP, Q), BF16),
             pltpu.VMEM((4, 2, NX, 8, 32, 256), F32),
             pltpu.VMEM((4, NX, 8, 32, 256), F32),
@@ -549,7 +578,7 @@
             pltpu.VMEM((4, 7, 4, 256), F32),
             dma, dma, dma((2, 4)), dma((CHUNKS,)), dma((7,)), dma, dma, dma((2, 4)), dma((GROUPS,)), dma((7,)),
             dma((4,)), dma((4,)), dma((4, 2, 2, 4)), dma((4, 2, 2, 4)),
-            dma((4,)), dma((4,)), dma((4,)), dma((4,)), dma,
+            dma((4,)), dma((4,)), dma((4,)), dma((4,)), dma, dma((2,)), dma,
         ],
         compiler_params=pltpu.CompilerParams(
             collective_id=0, has_side_effects=True, vmem_limit_bytes=58 * 1024 * 1024

time: 151 us -> 156 us (1.033)
  Pallas kernels: 149 us -> 154 us
    pallas_call x1, Pallas kernels: 144 us -> 150 us  [shards(): pl.pallas_call(kernel, out_shape=(jax.ShapeDtypeStruct((Q, D), F32), jax....]
where the time goes in v5:
time: 156 us; the launch traced here: 155 us
  Pallas kernels  154 us (99%)
    pallas_call x1, Pallas kernels, shards(): pl.pallas_call(kernel, out_shape=(jax.ShapeDtypeStruct((Q, D), F32), jax....  150 us

profile of v5, /device:TPU:1, one launch (start us, length us, event | category | flops | bytes accessed | tf_op | source)
XLA Modules:
  0.0 154.8 jit_solution(8028919316431007451)
XLA Ops:
  0.6 2.8 %shard_map.68 = (s32[8,16,1,128]{3,2,1,0:T(1,128)}, s32[8,128]{1,0:T(8,128)}) custom-call(s32[7,128]{1,0:T(8,128)} %bitcast.2), custom_call_target="tpu_custom_call" | custom-call | tf_op jit(solution)/shard_map/pallas_call | solution.py:532
  3.4 149.5 %shard_map.69 = (f32[128,1024]{1,0:T(8,128)}, f32[4,1024]{1,0:T(4,128)}) custom-call(s32[8,16,1,128]{3,2,1,0:T(1,128)} %get-tuple-element.6.req, s32[8,128]{1,0:T(8,128)} %get-tuple-element.7.slots, s32[1,128]{1,0:T(1,128)} %bitcast.3, bf16[4,1024]{1,0:T(4,128)(2,1)} %pas_ref.1, bf16[128,1024]{1,0:T(8,128)(2,1)} %q_ref.1, bf16[896,1024]{1,0:T(8,128)(2,1)} %neg_ref.1), custom_call_target="tpu_custom_call" | custom-call | flops 2147483648 | bytes 16777216 | tf_op jit(solution)/shard_map/pallas_call | solution.py:541
  152.9 1.9 %shard_map.70 = (f32[128,1024]{1,0:T(8,128)}, f32[4,1024]{1,0:T(4,128)}) custom-call(f32[128,1024]{1,0:T(8,128)} %get-tuple-element.8.gq_in, f32[4,1024]{1,0:T(4,128)} %get-tuple-element.9.gp_in), custom_call_target="tpu_custom_call" | custom-call | tf_op jit(solution)/shard_map/pallas_call | solution.py:588

commit v6 on v4

--- a/solution.py
+++ b/solution.py
@@ -85,8 +85,8 @@
     req, slots, pos_ref, pas_ref, q_ref, neg_ref,
     gq_ref, gp_ref,
     asked, passed, reqin, idsm, tab, g, f, fs, fn, st, hs, pst, pmine, zbuf, zf, pall,
-    wt, gpb, rc, r1x, r1a, ax, aa, r2x, r2a, a3, r3,
-    s_req, s_pass, s_y, s_row, s_ag, r_req, r_pass, r_y, r_row, r_ag, s_rc, r_rc, s_1, r_1, s_2, r_2, s_3, r_3, s_loc,
+    qall, wt, wk, acc2, r1, a3, r3,
+    s_req, s_pass, s_y, s_row, s_ag, r_req, r_pass, r_y, r_row, r_ag, s_q, r_q, s_w, r_w, s_1, r_1, s_3, r_3, s_loc,
 ):
     mb = lax.axis_index("blk")
     mg = lax.axis_index("grp")
@@ -111,6 +111,8 @@
     for i in range(NYL):
         greet(device(x, (1 - yh) * NYL + i, z, core))
     greet(sibling)
+    for i in range(1, NX):
+        greet(device((x + i) % NX, y, z, 1 - core))
 
     for c in range(C8):
         pst[pl.ds(c, 4, stride=C8), :] = pas_ref[:, c * 128:(c + 1) * 128].astype(F32)
@@ -118,7 +120,7 @@
     pmine[...] = own
     zbuf[z] = own
 
-    pl.semaphore_wait(barrier, NZ - 1 + 15 + NYL + 1)
+    pl.semaphore_wait(barrier, NZ - 1 + 15 + NYL + 1 + NX - 1)
 
     for i in range(1, NZ):
         rcopy(req.at[i], asked.at[i], s_req, r_req, (mb ^ i, mg)).start()
@@ -261,6 +263,22 @@
         rcopy(ref, ref, s_pass, r_row.at[group], sibling).wait_recv()
         return hard(group, top)
 
+    own_slot = core * NX + x
+    own_rows = qall.at[pl.ds(pl.multiple_of(own_slot * Q, Q), Q)]
+    own_rows[...] = q_ref[...]
+
+    def queries_x():
+        for i in range(1, NX):
+            to = device((x + i) % NX, y, z, core)
+            rcopy(own_rows, own_rows, s_q.at[0], r_q.at[0], to).start()
+
+    side_rows = qall.at[pl.ds(pl.multiple_of(core * NX * Q, NX * Q), NX * Q)]
+
+    def queries_across():
+        ref = qall.at[pl.ds(0, (NX - 1) * Q)]
+        rcopy(ref, ref, s_q.at[0], r_q.at[0], sibling).wait_recv()
+        rcopy(side_rows, side_rows, s_q.at[1], r_q.at[1], sibling).start()
+
     hard_top = jnp.full((1, Q), NEG, F32)
     along_y(1)
     for chunk in range(CHUNKS):
@@ -276,8 +294,11 @@
             along_x(1)
         elif chunk == 7:
             across()
+            queries_x()
         elif chunk == 10:
             pool_top, pool_total = pool()
+        elif chunk == 13:
+            queries_across()
         if chunk >= 5 and chunk % 2 == 1:
             hard_top = group_in((chunk - 5) // 2, hard_top)
     for group in range((CHUNKS - 4) // 2, GROUPS):
@@ -301,35 +322,19 @@
     source = (((there >> 2) & 7) << 5) | ((there >> 5) << 2) | (there & 3)
     swap = (iota((256, 256), 1) == source).astype(F32).astype(BF16)
 
-    def weigh(side):
-        def one(i, _):
-            at = pl.multiple_of(side * 1024 + i * 256, 256)
-            hit = (iota((256, Q), 0) + at == answer_slot).astype(F32)
-            w = st[pl.ds(at, 256), :] * factor - hit
-            st[pl.ds(at, 256), :] = w
-            w = w.astype(BF16)
-            wt[0, pl.ds(at, 256), :] = w
-            wt[1, pl.ds(at, 256), :] = mm(swap, w).astype(BF16)
-            return 0
-
-        lax.fori_loop(0, NX, one, 0)
-
-    def grads(j, side):
-        def one(i, _):
-            at = pl.multiple_of(side * 1024 + i * 256, 256)
-            part = mm(wt[j // 2, pl.ds(at, 256), :], q_ref[:, j * 256:(j + 1) * 256])
-            gpb[j, side, i] = part.reshape(8, 32, 256)
-            return 0
-
-        lax.fori_loop(0, NX, one, 0)
-
-    order = (1, 3, 0, 2)
-    weigh(1 - core)
-    for j in order:
-        grads(j, 1 - core)
-        rcopy(gpb.at[j, 1 - core], rc.at[j], s_rc.at[j], r_rc.at[j], sibling).start()
-    weigh(core)
-    grads(order[0], core)
+    def weigh(tile):
+        at = pl.multiple_of(tile * 256, 256)
+        hit = (iota((256, Q), 0) + at == answer_slot).astype(F32)
+        w = st[pl.ds(at, 256), :] * factor - hit
+        st[pl.ds(at, 256), :] = w
+        return w.astype(BF16)
+
+    for dc, dx in ((1, 2), (0, 2), (1, 1), (1, 3), (0, 1), (0, 3), (1, 0)):
+        tc, tx = (core + dc) % 2, (x + dx) % NX
+        tile = tc * NX + tx
+        wt[tile] = weigh(tile)
+        rcopy(wt.at[tile], wk.at[own_slot], s_w, r_w, device(tx, y, z, tc)).start()
+    wk[own_slot] = weigh(own_slot)
 
     def along(axis, i):
         return (
@@ -338,68 +343,48 @@
             else device(x, y, (z + i + NZ) % NZ, core)
         )
 
-    where = {"x": x, "y": y, "z": z}
-
-    def ring(j):
-        axis = "xyxz"[j]
-        n = NX if axis == "x" else 8
-        o = j // 2
-
-        def own(half, target):
-            t = (where[axis] + target + n) % n
-            if axis == "x":
-                return gpb.at[j, core, t, pl.ds(half * 4, 4)]
-            return gpb.at[j, core, pl.ds(half * 2, 2), t]
-
-        def held(half, way, hop):
-            return (r1x if axis == "x" else r1a).at[o, half, way, hop]
-
-        def hops(half, way):
-            return n // 2 if half == way else n // 2 - 1
-
-        return axis, own, held, hops
-
-    def send(j, hop):
-        axis, own, held, hops = ring(j)
-        for half in range(2):
-            for way in range(2):
-                length, sign = hops(half, way), 1 - 2 * way
-                if hop >= length:
-                    continue
-                if hop == 0:
-                    source = own(half, sign * length)
-                else:
-                    source = held(half, way, hop - 1)
-                    rcopy(
-                        source, source, s_1.at[j, half, way, hop - 1], r_1.at[j, half, way, hop - 1], sibling
-                    ).wait_recv()
-                    source[...] = source[...] + own(half, sign * (length - hop))[...]
+    where = {"y": y, "z": z}
+
+    def own(o, half, target):
+        return acc2.at[o, (where["yz"[o]] + target + 8) % 8, pl.ds(half * 16, 16)]
+
+    def hops(half, way):
+        return 4 if half == way else 3
+
+    def send(o, hop):
+        for half, way in ((0, 0), (1, 1), (1, 0), (0, 1)):
+            length, sign = hops(half, way), 1 - 2 * way
+            if hop >= length:
+                continue
+            if hop == 0:
+                source = own(o, half, sign * length)
+            else:
+                source = r1.at[o, half, way, hop - 1]
                 rcopy(
-                    source, held(half, way, hop), s_1.at[j, half, way, hop], r_1.at[j, half, way, hop],
-                    along(axis, sign),
-                ).start()
-
-    def arrived(j, half):
-        axis, own, held, hops = ring(j)
-        acc = own(half, 0)[...]
+                    source, source, s_1.at[o, half, way, hop - 1], r_1.at[o, half, way, hop - 1], sibling
+                ).wait_recv()
+                source[...] = source[...] + own(o, half, sign * (length - hop))[...]
+            rcopy(
+                source, r1.at[o, half, way, hop], s_1.at[o, half, way, hop], r_1.at[o, half, way, hop],
+                along("yz"[o], sign),
+            ).start()
+
+    def arrived(o, half):
+        acc = own(o, half, 0)[...]
         for way in range(2):
             hop = hops(half, way) - 1
-            ref = held(half, way, hop)
-            rcopy(ref, ref, s_1.at[j, half, way, hop], r_1.at[j, half, way, hop], sibling).wait_recv()
+            ref = r1.at[o, half, way, hop]
+            rcopy(ref, ref, s_1.at[o, half, way, hop], r_1.at[o, half, way, hop], sibling).wait_recv()
             acc = acc + ref[...]
         return acc
 
-    for place, j in enumerate(order):
-        if place:
-            grads(j, core)
-        rcopy(gpb.at[j, 1 - core], rc.at[j], s_rc.at[j], r_rc.at[j], sibling).wait_recv()
-
-        def add(i, _, j=j):
-            gpb[j, core, i] = gpb[j, core, i] + rc[j, i]
-            return 0
-
-        lax.fori_loop(0, NX, add, 0)
-        send(j, 0)
+    def tile_sums(o):
+        weights = jnp.concatenate([wk[i] for i in range(8)], axis=1)
+        if o:
+            weights = mm(swap, weights).astype(BF16)
+        for n in range(2):
+            part = mm(weights, qall[:, o * 512 + n * 256:o * 512 + (n + 1) * 256])
+            acc2[o, :, :, n * 256:(n + 1) * 256] = part.reshape(8, 32, 256)
 
     def queries_half(half_at):
         cols = slice(half_at * 512, (half_at + 1) * 512)
@@ -419,58 +404,35 @@
         gq_ref[:, cols] = acc
 
     queries_half(0)
-    for j in order:
-        send(j, 1)
+    rcopy(side_rows, side_rows, s_q.at[1], r_q.at[1], sibling).wait_recv()
+    rcopy(wk.at[pl.ds(0, 7)], wk.at[pl.ds(0, 7)], s_w, r_w, sibling).wait_recv()
+    tile_sums(0)
+    send(0, 0)
+    tile_sums(1)
+    send(1, 0)
     queries_half(1)
-    for j in (1, 3):
-        send(j, 2)
-    for j in (0, 2):
-        o = j // 2
-        a = "yz"[o]
+    for hop in range(1, 4):
+        send(0, hop)
+        send(1, hop)
+
+    for o in range(2):
+        b = "zy"[o]
         for half in range(2):
-            ax[o, pl.ds(half * 4, 4)] = arrived(j, half)
+            acc = arrived(o, half)
+            for i in range(4):
+                a3[o, half * 4 + i] = acc[i * 4:(i + 1) * 4, :]
         for i in range(1, 8):
             rcopy(
-                ax.at[o, (where[a] + i) % 8], r2a.at[o, i - 1], s_2.at[j], r_2.at[j], along(a, i)
+                a3.at[o, (where[b] + i) % 8], r3.at[o, i - 1], s_3.at[o], r_3.at[o], along(b, i)
             ).start()
-    for j in (1, 3):
-        send(j, 3)
-    for j in (1, 3):
-        o = j // 2
-        for half in range(2):
-            aa[o, pl.ds(half * 2, 2)] = arrived(j, half)
-        for i in range(1, NX):
-            rcopy(
-                aa.at[o, (x + i) % NX], r2x.at[o, i - 1], s_2.at[j], r_2.at[j], along("x", i)
-            ).start()
-
-    for j in (0, 2, 1, 3):
-        o, first_x = j // 2, j % 2 == 0
-        a, b = "yz"[o], "zy"[o]
-        if first_x:
-            rcopy(r2a.at[o], r2a.at[o], s_2.at[j], r_2.at[j], sibling).wait_recv()
-            acc = ax[o, where[a]]
-            for i in range(7):
-                acc = acc + r2a[o, i]
-        else:
-            rcopy(r2x.at[o], r2x.at[o], s_2.at[j], r_2.at[j], sibling).wait_recv()
-            acc = aa[o, x]
-            for i in range(NX - 1):
-                acc = acc + r2x[o, i]
-        for i in range(8):
-            a3[j, i] = acc[i * 4:(i + 1) * 4, :]
-        for i in range(1, 8):
-            rcopy(
-                a3.at[j, (where[b] + i) % 8], r3.at[j, i - 1], s_3.at[j], r_3.at[j], along(b, i)
-            ).start()
-
-    for j in range(4):
-        b = "zy"[j // 2]
-        rcopy(r3.at[j], r3.at[j], s_3.at[j], r_3.at[j], sibling).wait_recv()
-        acc = a3[j, where[b]]
+
+    for o in range(2):
+        b = "zy"[o]
+        rcopy(r3.at[o], r3.at[o], s_3.at[o], r_3.at[o], sibling).wait_recv()
+        acc = a3[o, where[b]]
         for i in range(7):
-            acc = acc + r3[j, i]
-        gp_ref[:, j * 256:(j + 1) * 256] = acc
+            acc = acc + r3[o, i]
+        gp_ref[:, o * 512:(o + 1) * 512] = acc
 
     def left(ref, sem):
         rcopy(ref, ref, sem, sem, sibling).wait_send()
@@ -487,16 +449,15 @@
         left(pall.at[pl.ds(0, 256)], s_ag.at[2 + n])
         left(pall.at[pl.ds(0, 128)], s_ag.at[4 + n])
     left(pall.at[pl.ds(0, 1024)], s_ag.at[6])
-    for j in range(4):
-        o, first_x = j // 2, j % 2 == 0
-        left(rc.at[j], s_rc.at[j])
-        _, _, held, hops = ring(j)
+    left(qall.at[pl.ds(0, (NX - 1) * Q)], s_q.at[0])
+    left(side_rows, s_q.at[1])
+    left(wk.at[pl.ds(0, 7)], s_w)
+    for o in range(2):
         for half in range(2):
             for way in range(2):
                 for hop in range(hops(half, way)):
-                    left(held(half, way, hop), s_1.at[j, half, way, hop])
-        left(r2a.at[o] if first_x else r2x.at[o], s_2.at[j])
-        left(r3.at[j], s_3.at[j])
+                    left(r1.at[o, half, way, hop], s_1.at[o, half, way, hop])
+        left(r3.at[o], s_3.at[o])
 
 
 def shards(queries, passages, negatives, neg_ids, positives):
@@ -536,20 +497,16 @@
             pltpu.VMEM((NZ, 32, 128), BF16),
             pltpu.VMEM((NZ * 32, 128), F32),
             pltpu.VMEM((NP, D), BF16),
-            pltpu.VMEM((2, NP, Q), BF16),
-            pltpu.VMEM((4, 2, NX, 8, 32, 256), F32),
-            pltpu.VMEM((4, NX, 8, 32, 256), F32),
-            pltpu.VMEM((2, 2, 2, 2, 4, 32, 256), F32),
-            pltpu.VMEM((2, 2, 2, 4, 2, 32, 256), F32),
-            pltpu.VMEM((2, 8, 32, 256), F32),
-            pltpu.VMEM((2, NX, 32, 256), F32),
-            pltpu.VMEM((2, NX - 1, 32, 256), F32),
-            pltpu.VMEM((2, 7, 32, 256), F32),
-            pltpu.VMEM((4, 8, 4, 256), F32),
-            pltpu.VMEM((4, 7, 4, 256), F32),
+            pltpu.VMEM((8 * Q, D), BF16),
+            pltpu.VMEM((8, 256, Q), BF16),
+            pltpu.VMEM((8, 256, Q), BF16),
+            pltpu.VMEM((2, 8, 32, 512), F32),
+            pltpu.VMEM((2, 2, 2, 4, 16, 512), F32),
+            pltpu.VMEM((2, 8, 4, 512), F32),
+            pltpu.VMEM((2, 7, 4, 512), F32),
             dma, dma, dma((2, 4)), dma((CHUNKS,)), dma((7,)), dma, dma, dma((2, 4)), dma((GROUPS,)), dma((7,)),
-            dma((4,)), dma((4,)), dma((4, 2, 2, 4)), dma((4, 2, 2, 4)),
-            dma((4,)), dma((4,)), dma((4,)), dma((4,)), dma,
+            dma((2,)), dma((2,)), dma, dma,
+            dma((2, 2, 2, 4)), dma((2, 2, 2, 4)), dma((2,)), dma((2,)), dma,
         ],
         compiler_params=pltpu.CompilerParams(
             collective_id=0, has_side_effects=True, vmem_limit_bytes=58 * 1024 * 1024

time: 151 us -> 138 us (0.914)
  Pallas kernels: 149 us -> 136 us
    pallas_call x1, Pallas kernels: 144 us -> 131 us  [shards(): pl.pallas_call(kernel, out_shape=(jax.ShapeDtypeStruct((Q, D), F32), jax....]
where the time goes in v6:
time: 138 us; the launch traced here: 137 us
  Pallas kernels  136 us (99%)
    pallas_call x1, Pallas kernels, shards(): pl.pallas_call(kernel, out_shape=(jax.ShapeDtypeStruct((Q, D), F32), jax....  131 us
    pallas_call x1, Pallas kernels, shards(): pl.pallas_call(requests, out_shape=(jax.ShapeDtypeStruct((NZ, 16, 1, 128)...  2.78 us

profile of v6, /device:TPU:1, one launch (start us, length us, event | category | flops | bytes accessed | tf_op | source)
XLA Modules:
  0.0 136.6 jit_solution(12094994351400742859)
XLA Ops:
  0.6 2.8 %shard_map.68 = (s32[8,16,1,128]{3,2,1,0:T(1,128)}, s32[8,128]{1,0:T(8,128)}) custom-call(s32[7,128]{1,0:T(8,128)} %bitcast.2), custom_call_target="tpu_custom_call" | custom-call | tf_op jit(solution)/shard_map/pallas_call | solution.py:466
  3.4 131.3 %shard_map.69 = (f32[128,1024]{1,0:T(8,128)}, f32[4,1024]{1,0:T(4,128)}) custom-call(s32[8,16,1,128]{3,2,1,0:T(1,128)} %get-tuple-element.6.req, s32[8,128]{1,0:T(8,128)} %get-tuple-element.7.slots, s32[1,128]{1,0:T(1,128)} %bitcast.3, bf16[4,1024]{1,0:T(4,128)(2,1)} %pas_ref.1, bf16[128,1024]{1,0:T(8,128)(2,1)} %q_ref.1, bf16[896,1024]{1,0:T(8,128)(2,1)} %neg_ref.1), custom_call_target="tpu_custom_call" | custom-call | flops 2147483648 | bytes 16777216 | tf_op jit(solution)/shard_map/pallas_call | solution.py:475
  134.8 1.9 %shard_map.70 = (f32[128,1024]{1,0:T(8,128)}, f32[4,1024]{1,0:T(4,128)}) custom-call(f32[128,1024]{1,0:T(8,128)} %get-tuple-element.8.gq_in, f32[4,1024]{1,0:T(4,128)} %get-tuple-element.9.gp_in), custom_call_target="tpu_custom_call" | custom-call | tf_op jit(solution)/shard_map/pallas_call | solution.py:516

commit v7 on v6

--- a/solution.py
+++ b/solution.py
@@ -85,8 +85,8 @@
     req, slots, pos_ref, pas_ref, q_ref, neg_ref,
     gq_ref, gp_ref,
     asked, passed, reqin, idsm, tab, g, f, fs, fn, st, hs, pst, pmine, zbuf, zf, pall,
-    qall, wt, wk, acc2, r1, a3, r3,
-    s_req, s_pass, s_y, s_row, s_ag, r_req, r_pass, r_y, r_row, r_ag, s_q, r_q, s_w, r_w, s_1, r_1, s_3, r_3, s_loc,
+    qall, posall, lseall, ts, wn, wh, wk, acc2, r1, a3, r3,
+    s_req, s_pass, s_y, s_row, s_ag, r_req, r_pass, r_y, r_row, r_ag, s_q, r_q, s_w, r_w, s_p, r_p, s_1, r_1, s_3, r_3, s_loc,
 ):
     mb = lax.axis_index("blk")
     mg = lax.axis_index("grp")
@@ -263,14 +263,33 @@
         rcopy(ref, ref, s_pass, r_row.at[group], sibling).wait_recv()
         return hard(group, top)
 
+    p = pos_ref[...]
+    answer_slot = (
+        (((p >> 2) & 1) << 10)
+        | (((p >> 7) & 3) << 8)
+        | (((p >> 3) & 1) << 7)
+        | (((p >> 9) & 3) << 5)
+        | (((p >> 4) & 7) << 2)
+        | (p & 3)
+    )
     own_slot = core * NX + x
     own_rows = qall.at[pl.ds(pl.multiple_of(own_slot * Q, Q), Q)]
     own_rows[...] = q_ref[...]
+    posall[own_slot] = jnp.broadcast_to(answer_slot, (8, Q))
+
+    def to_eight(ref, s_sem, r_sem):
+        for dc, dx in ((1, 2), (0, 2), (1, 1), (1, 3), (0, 1), (0, 3), (1, 0)):
+            to = device((x + dx) % NX, y, z, (core + dc) % 2)
+            rcopy(ref.at[own_slot], ref.at[own_slot], s_sem, r_sem, to).start()
+
+    def from_eight(ref, s_sem, r_sem):
+        rcopy(ref.at[pl.ds(0, 7)], ref.at[pl.ds(0, 7)], s_sem, r_sem, sibling).wait_recv()
 
     def queries_x():
         for i in range(1, NX):
             to = device((x + i) % NX, y, z, core)
             rcopy(own_rows, own_rows, s_q.at[0], r_q.at[0], to).start()
+        to_eight(posall, s_p, r_p)
 
     side_rows = qall.at[pl.ds(pl.multiple_of(core * NX * Q, NX * Q), NX * Q)]
 
@@ -278,6 +297,16 @@
         ref = qall.at[pl.ds(0, (NX - 1) * Q)]
         rcopy(ref, ref, s_q.at[0], r_q.at[0], sibling).wait_recv()
         rcopy(side_rows, side_rows, s_q.at[1], r_q.at[1], sibling).start()
+
+    def tile_scores():
+        rcopy(side_rows, side_rows, s_q.at[1], r_q.at[1], sibling).wait_recv()
+
+        def one(i, _):
+            tile = pall[pl.ds(pl.multiple_of(own_slot * 256, 256), 256), :]
+            ts[i] = nt(tile, qall[pl.ds(pl.multiple_of(i * Q, Q), Q), :]) * SCALE
+            return 0
+
+        lax.fori_loop(0, 8, one, 0)
 
     hard_top = jnp.full((1, Q), NEG, F32)
     along_y(1)
@@ -294,11 +323,14 @@
             along_x(1)
         elif chunk == 7:
             across()
-            queries_x()
         elif chunk == 10:
             pool_top, pool_total = pool()
-        elif chunk == 13:
+        elif chunk == 6:
+            queries_x()
+        elif chunk == 12:
             queries_across()
+        elif chunk == 15:
+            tile_scores()
         if chunk >= 5 and chunk % 2 == 1:
             hard_top = group_in((chunk - 5) // 2, hard_top)
     for group in range((CHUNKS - 4) // 2, GROUPS):
@@ -309,32 +341,36 @@
     lse = top + jnp.log(total)
     factor = jnp.exp(pool_top - lse)
 
-    p = pos_ref[...]
-    answer_slot = (
-        (((p >> 2) & 1) << 10)
-        | (((p >> 7) & 3) << 8)
-        | (((p >> 3) & 1) << 7)
-        | (((p >> 9) & 3) << 5)
-        | (((p >> 4) & 7) << 2)
-        | (p & 3)
-    )
     there = iota((256, 256), 0)
     source = (((there >> 2) & 7) << 5) | ((there >> 5) << 2) | (there & 3)
     swap = (iota((256, 256), 1) == source).astype(F32).astype(BF16)
 
-    def weigh(tile):
-        at = pl.multiple_of(tile * 256, 256)
+    lseall[own_slot] = jnp.broadcast_to(lse, (8, Q))
+    to_eight(lseall, s_w, r_w)
+
+    def turn(t, _):
+        at = pl.multiple_of(t * 256, 256)
         hit = (iota((256, Q), 0) + at == answer_slot).astype(F32)
         w = st[pl.ds(at, 256), :] * factor - hit
-        st[pl.ds(at, 256), :] = w
-        return w.astype(BF16)
-
-    for dc, dx in ((1, 2), (0, 2), (1, 1), (1, 3), (0, 1), (0, 3), (1, 0)):
-        tc, tx = (core + dc) % 2, (x + dx) % NX
-        tile = tc * NX + tx
-        wt[tile] = weigh(tile)
-        rcopy(wt.at[tile], wk.at[own_slot], s_w, r_w, device(tx, y, z, tc)).start()
-    wk[own_slot] = weigh(own_slot)
+        wn[:, pl.ds(at, 256)] = jnp.transpose(w).astype(BF16)
+        return 0
+
+    def turn_hard(t, _):
+        at = pl.multiple_of(t * 256, 256)
+        w = jnp.exp(hs[pl.ds(at, 256), :] - lse)
+        wh[:, pl.ds(at, 256)] = jnp.transpose(w).astype(BF16)
+        return 0
+
+    lax.fori_loop(0, NP // 256, turn, 0)
+    from_eight(posall, s_p, r_p)
+    from_eight(lseall, s_w, r_w)
+
+    def weigh(i, _):
+        hit = (iota((256, Q), 0) + own_slot * 256 == posall[i, 0:1, :]).astype(F32)
+        wk[i] = (jnp.exp(ts[i] - lseall[i, 0:1, :]) - hit).astype(BF16)
+        return 0
+
+    lax.fori_loop(0, 8, weigh, 0)
 
     def along(axis, i):
         return (
@@ -391,27 +427,26 @@
 
         def passages(t, acc):
             at = pl.multiple_of(t * 256, 256)
-            w = jnp.transpose(st[pl.ds(at, 256), :]).astype(BF16)
-            return acc + mm(w, pall[pl.ds(at, 256), cols])
+            return acc + mm(wn[:, pl.ds(at, 256)], pall[pl.ds(at, 256), cols])
 
         def negatives(t, acc):
             at = pl.multiple_of(t * 256, 256)
-            w = jnp.transpose(jnp.exp(hs[pl.ds(at, 256), :] - lse)).astype(BF16)
-            return acc + mm(w, fn[pl.ds(at, 256), cols])
+            return acc + mm(wh[:, pl.ds(at, 256)], fn[pl.ds(at, 256), cols])
 
         acc = lax.fori_loop(0, NP // 256, passages, jnp.zeros((Q, 512), F32))
         acc = lax.fori_loop(0, SLOTS // 256, negatives, acc)
         gq_ref[:, cols] = acc
 
-    queries_half(0)
-    rcopy(side_rows, side_rows, s_q.at[1], r_q.at[1], sibling).wait_recv()
-    rcopy(wk.at[pl.ds(0, 7)], wk.at[pl.ds(0, 7)], s_w, r_w, sibling).wait_recv()
     tile_sums(0)
     send(0, 0)
     tile_sums(1)
     send(1, 0)
+    lax.fori_loop(0, SLOTS // 256, turn_hard, 0)
+    queries_half(0)
+    send(0, 1)
+    send(1, 1)
     queries_half(1)
-    for hop in range(1, 4):
+    for hop in range(2, 4):
         send(0, hop)
         send(1, hop)
 
@@ -451,7 +486,8 @@
     left(pall.at[pl.ds(0, 1024)], s_ag.at[6])
     left(qall.at[pl.ds(0, (NX - 1) * Q)], s_q.at[0])
     left(side_rows, s_q.at[1])
-    left(wk.at[pl.ds(0, 7)], s_w)
+    left(lseall.at[pl.ds(0, 7)], s_w)
+    left(posall.at[pl.ds(0, 7)], s_p)
     for o in range(2):
         for half in range(2):
             for way in range(2):
@@ -498,14 +534,18 @@
             pltpu.VMEM((NZ * 32, 128), F32),
             pltpu.VMEM((NP, D), BF16),
             pltpu.VMEM((8 * Q, D), BF16),
-            pltpu.VMEM((8, 256, Q), BF16),
+            pltpu.VMEM((8, 8, Q), I32),
+            pltpu.VMEM((8, 8, Q), F32),
+            pltpu.VMEM((8, 256, Q), F32),
+            pltpu.VMEM((Q, NP), BF16),
+            pltpu.VMEM((Q, SLOTS), BF16),
             pltpu.VMEM((8, 256, Q), BF16),
             pltpu.VMEM((2, 8, 32, 512), F32),
             pltpu.VMEM((2, 2, 2, 4, 16, 512), F32),
             pltpu.VMEM((2, 8, 4, 512), F32),
             pltpu.VMEM((2, 7, 4, 512), F32),
             dma, dma, dma((2, 4)), dma((CHUNKS,)), dma((7,)), dma, dma, dma((2, 4)), dma((GROUPS,)), dma((7,)),
-            dma((2,)), dma((2,)), dma, dma,
+            dma((2,)), dma((2,)), dma, dma, dma, dma,
             dma((2, 2, 2, 4)), dma((2, 2, 2, 4)), dma((2,)), dma((2,)), dma,
         ],
         compiler_params=pltpu.CompilerParams(

time: 138 us -> 134 us (0.971)
  Pallas kernels: 136 us -> 131 us
    pallas_call x1, Pallas kernels: 131 us -> 127 us  [shards(): pl.pallas_call(kernel, out_shape=(jax.ShapeDtypeStruct((Q, D), F32), jax....]
where the time goes in v7:
time: 134 us; the launch traced here: 132 us
  Pallas kernels  131 us (98%)
    pallas_call x1, Pallas kernels, shards(): pl.pallas_call(kernel, out_shape=(jax.ShapeDtypeStruct((Q, D), F32), jax....  127 us
    pallas_call x1, Pallas kernels, shards(): pl.pallas_call(requests, out_shape=(jax.ShapeDtypeStruct((NZ, 16, 1, 128)...  2.78 us

profile of v7, /device:TPU:1, one launch (start us, length us, event | category | flops | bytes accessed | tf_op | source)
XLA Modules:
  0.0 131.9 jit_solution(15948122465476089968)
XLA Ops:
  0.6 2.8 %shard_map.68 = (s32[8,16,1,128]{3,2,1,0:T(1,128)}, s32[8,128]{1,0:T(8,128)}) custom-call(s32[7,128]{1,0:T(8,128)} %bitcast.2), custom_call_target="tpu_custom_call" | custom-call | tf_op jit(solution)/shard_map/pallas_call | solution.py:502
  3.4 126.6 %shard_map.69 = (f32[128,1024]{1,0:T(8,128)}, f32[4,1024]{1,0:T(4,128)}) custom-call(s32[8,16,1,128]{3,2,1,0:T(1,128)} %get-tuple-element.6.req, s32[8,128]{1,0:T(8,128)} %get-tuple-element.7.slots, s32[1,128]{1,0:T(1,128)} %bitcast.3, bf16[4,1024]{1,0:T(4,128)(2,1)} %pas_ref.1, bf16[128,1024]{1,0:T(8,128)(2,1)} %q_ref.1, bf16[896,1024]{1,0:T(8,128)(2,1)} %neg_ref.1), custom_call_target="tpu_custom_call" | custom-call | flops 2147483648 | bytes 16777216 | tf_op jit(solution)/shard_map/pallas_call | solution.py:511
  130.0 1.9 %shard_map.70 = (f32[128,1024]{1,0:T(8,128)}, f32[4,1024]{1,0:T(4,128)}) custom-call(f32[128,1024]{1,0:T(8,128)} %get-tuple-element.8.gq_in, f32[4,1024]{1,0:T(4,128)} %get-tuple-element.9.gp_in), custom_call_target="tpu_custom_call" | custom-call | tf_op jit(solution)/shard_map/pallas_call | solution.py:556
